TPU v7x, 128 devices: a whole 4x4x4 slice. The times are simulated.
128 devices in a mesh: row: 4 (over z_hi, core), col: 32 (over y, x, z_lo).
Axes of the slice: x: 4, y: 4, z: 4 (z_hi: 2, z_lo: 2; z = z_hi * 2 + z_lo), core: 2. Of those that a mesh axis runs over, the one named last changes fastest.
Arguments:
- field: bfloat16 [128, 2048, 512], P('row', 'col'), may hold values from -6 to 6
- w_expand: bfloat16 [512, 2048], replicated, may hold values from -0.25 to 0.25
- dw_kernel: float32 [3, 3, 2048], replicated, may hold values from -2 to 2
- w_project: bfloat16 [2048, 512], replicated, may hold values from -0.125 to 0.125
- qkv_block: bfloat16 [512, 1536], replicated, may hold values from -5 to 5
- out_block: bfloat16 [512, 512], replicated, may hold values from -0.25 to 0.25
- qkv_grid: bfloat16 [512, 1536], replicated, may hold values from -5 to 5
- out_grid: bfloat16 [512, 512], replicated, may hold values from -0.25 to 0.25
Outputs:
- result: bfloat16 [128, 2048, 512], P('row', 'col')
All inputs are finite; a program needn't handle non-finite values.
Results may differ from a plain program's by a relative error of at most 0.011.
Values may be sent and summed in bfloat16 or wider, within the bound.
No kernel may reach another device: no remote copies, remote signals or barrier semaphores. Data moves between devices by JAX's collectives and lax.ppermute only.
A program may use at most 128 MiB of HBM per device.

v0:
```python
import functools

import jax
import jax.numpy as jnp
import numpy as np
from jax import lax
from jax.experimental import pallas as pl
from jax.experimental.pallas import tpu as pltpu
from jax.sharding import PartitionSpec as P

BF16 = jnp.bfloat16
F32 = jnp.float32
HEAD = 32
CHANS = 512
WIDE = 2048
CB = 1024
BLOCKS = WIDE // CB
PAIRS = 4
VMEM_LIMIT = 28 * 2**20
SCALE_LOG2 = float(HEAD**-0.5 * np.log2(np.e))


def layer_norm(v):
    mean = jnp.mean(v, axis=-1, keepdims=True)
    cent = v - mean
    var = jnp.mean(cent * cent, axis=-1, keepdims=True)
    return (cent * lax.rsqrt(var + 1e-05)).astype(BF16)


def gelu(v):
    half = 0.5 * v
    return half + half * lax.erf(v * 0.7071067811865476)


def mm(a, b):
    return lax.dot_general(a, b, (((1,), (0,)), ((), ())), preferred_element_type=F32)


def mm_nt(a, b):
    return lax.dot_general(a, b, (((1,), (1,)), ((), ())), preferred_element_type=F32)


def ones_where(shape, holds):
    row = lax.broadcasted_iota(jnp.int32, shape, 0)
    column = lax.broadcasted_iota(jnp.int32, shape, 1)
    return jnp.where(holds(row, column), 1.0, 0.0).astype(BF16)


def spread_matrix():
    return ones_where(
        (256, 256),
        lambda r, c: c == ((r >> 3) & 1) * 128 + (r >> 7) * 64 + (r & 7) * 8 + ((r >> 4) & 7),
    )


def turn_matrix():
    return ones_where((256, 256), lambda r, c: c == (r & 15) * 16 + (r >> 4))


def edge_matrix(part):
    def holds(r, c):
        j, b, q = r >> 4, (r >> 3) & 1, r & 7
        own = c == j * 16 + 8 * part + q
        rim = c == 128 + q * 8 + j
        return (own & (b == 1 - part)) | (rim & (b == part))

    return ones_where((128, 192), holds)


def head_mask():
    return ones_where((256, 128), lambda r, c: (r >> 6) == (c >> 5))


def in_vmem():
    return pl.BlockSpec(memory_space=pltpu.VMEM)


def in_hbm(count):
    return [pl.BlockSpec(memory_space=pltpu.HBM)] * count


def kept_in_hbm(*arrays):
    return [pltpu.with_memory_space_constraint(a, pltpu.HBM) for a in arrays]


def fetch(sems, *pairs):
    copies = [pltpu.make_async_copy(source, to, sems.at[at]) for at, (source, to) in enumerate(pairs)]
    for copy in copies:
        copy.start()
    return copies


def params():
    return pltpu.CompilerParams(vmem_limit_bytes=VMEM_LIMIT)


def segment_max(scores):
    low = lax.broadcasted_iota(jnp.int32, (1, 128), 1) < 64
    found = []
    for at in range(0, scores.shape[1], 128):
        v = scores[:, at : at + 128]
        first = jnp.max(jnp.where(low, v, -jnp.inf), axis=-1, keepdims=True)
        second = jnp.max(jnp.where(low, -jnp.inf, v), axis=-1, keepdims=True)
        found.append(jnp.where(low, first, second))
    return jnp.concatenate(found, axis=1)


def attention(grouped, wqkv_ref, wo_ref, mask_ref, proj, context, emit):
    mask = mask_ref[...]

    def one(half, carry):
        x = grouped[pl.ds(8 * half, 8)].reshape(512, CHANS).astype(F32)
        proj[...] = mm(layer_norm(x), wqkv_ref[...]).astype(BF16)
        for g in range(8):
            rows = slice(64 * g, 64 * g + 64)
            for at in range(0, CHANS, 128):
                query = proj[rows, at : at + 128]
                keys = jnp.concatenate([proj[rows, CHANS + at : CHANS + at + 128]] * 4, axis=0) * mask
                values = jnp.concatenate([proj[rows, 2 * CHANS + at : 2 * CHANS + at + 128]] * 4, axis=0) * mask
                scores = mm_nt(query, keys)
                weights = jnp.exp2((scores - segment_max(scores)) * SCALE_LOG2).astype(BF16)
                both = mm(weights, jnp.concatenate([values, mask], axis=1))
                context[rows, at : at + 128] = (both[:, :128] / both[:, 128:]).astype(BF16)
        emit(half, x + mm(context[...], wo_ref[...]))
        return carry

    lax.fori_loop(0, 2, one, 0, unroll=2)


def grid_kernel(x_ref, wqkv_ref, wo_ref, *rest):
    out_ref, grouped, proj, context, turn_ref, mask_ref = rest[-6:]
    turn_ref[...] = turn_matrix()
    mask_ref[...] = head_mask()
    for t in range(4):
        moved = mm(turn_ref[...], x_ref[16 * t : 16 * t + 16].reshape(256, CHANS))
        grouped[:, 16 * t : 16 * t + 16] = moved.astype(BF16).reshape(16, 16, CHANS)

    def emit(half, rows):
        grouped[pl.ds(8 * half, 8)] = rows.astype(BF16).reshape(8, 64, CHANS)

    attention(grouped, wqkv_ref, wo_ref, mask_ref, proj, context, emit)
    for t in range(4):
        moved = mm(turn_ref[...], grouped[:, 16 * t : 16 * t + 16].reshape(256, CHANS))
        moved = moved.astype(BF16).reshape(8, 2, 16, CHANS)
        if len(rest) == 6:
            out_ref[8 * t : 8 * t + 8] = moved
        else:
            out_ref[8 * t : 8 * t + 8, 1] = moved
    if len(rest) > 6:
        out_ref[:, 0] = rest[0][...]


def attention_scratch():
    return [
        pltpu.VMEM((16, 64, CHANS), BF16),
        pltpu.VMEM((512, 3 * CHANS), BF16),
        pltpu.VMEM((512, CHANS), BF16),
        pltpu.VMEM((256, 256), BF16),
        pltpu.VMEM((256, 128), BF16),
    ]


def grid_attention(x, qkv, out_proj, *earlier):
    shape = (32, 2, 2, 16, CHANS) if earlier else (32, 2, 16, CHANS)
    return pl.pallas_call(
        grid_kernel,
        in_specs=[in_vmem() for _ in range(3 + len(earlier))],
        out_specs=in_vmem(),
        out_shape=jax.ShapeDtypeStruct(shape, BF16),
        scratch_shapes=attention_scratch(),
        compiler_params=params(),
        cost_estimate=pl.CostEstimate(
            flops=8 * 1024 * CHANS * CHANS, bytes_accessed=4 * 2**20, transcendentals=2**20
        ),
        name="grid_attention",
    )(x, qkv, out_proj, *earlier)


def prepare_kernel(x_hbm, we_hbm, dw_hbm, wp_hbm, *rest):
    small_hbm, (_, normed_ref, xp_ref, we_ref, dw_ref, wp_ref), small, (x_ref, spread_ref, sems) = (
        rest[0:4], rest[4:10], rest[10:14], rest[14:],
    )
    rows = [
        fetch(sems.at[0, pl.ds(k, 1)], (x_hbm.at[:, 8 * k : 8 * k + 8], x_ref.at[:, 8 * k : 8 * k + 8]))[0]
        for k in range(2)
    ]
    copies = fetch(
        sems.at[1],
        *[(we_hbm.at[:, CB * s : CB * s + CB], we_ref.at[s]) for s in range(BLOCKS)],
        *[(dw_hbm.at[:, :, CB * s : CB * s + CB], dw_ref.at[s]) for s in range(BLOCKS)],
        *[(wp_hbm.at[CB * s : CB * s + CB], wp_ref.at[s]) for s in range(BLOCKS)],
        *zip(small_hbm, small),
    )
    spread_ref[...] = spread_matrix()
    for pair in range(8):
        if pair % 4 == 0:
            rows[pair // 4].wait()
        moved = mm(spread_ref[...], x_ref[:, 2 * pair : 2 * pair + 2].reshape(256, CHANS))
        xp_ref[256 * pair : 256 * pair + 256] = moved.astype(BF16)
        normed_ref[256 * pair : 256 * pair + 256] = layer_norm(moved)
    for copy in copies:
        copy.wait()


def prepare(after, field, w_expand, dw_kernel, w_project, *small):
    out_shape = [
        jax.ShapeDtypeStruct((2048, CHANS), BF16),
        jax.ShapeDtypeStruct((2048, CHANS), BF16),
        jax.ShapeDtypeStruct((BLOCKS, CHANS, CB), BF16),
        jax.ShapeDtypeStruct((BLOCKS, 3, 3, CB), F32),
        jax.ShapeDtypeStruct((BLOCKS, CB, CHANS), BF16),
        *[jax.ShapeDtypeStruct(a.shape, BF16) for a in small],
    ]
    return pl.pallas_call(
        prepare_kernel,
        in_specs=[*in_hbm(8), pl.BlockSpec(memory_space=pl.ANY)],
        out_specs=[in_vmem() for _ in out_shape],
        out_shape=out_shape,
        scratch_shapes=[
            pltpu.VMEM((2, 16, 64, CHANS), BF16),
            pltpu.VMEM((256, 256), BF16),
            pltpu.SemaphoreType.DMA((2, 4 + 3 * BLOCKS)),
        ],
        compiler_params=params(),
        cost_estimate=pl.CostEstimate(flops=10**10, bytes_accessed=16 * 2**20, transcendentals=0),
        name="prepare",
    )(*kept_in_hbm(field.reshape(2, 16, 64, CHANS), w_expand, dw_kernel, w_project, *small), after)


def local_kernel(
    part, rim_ref, left_ref, right_ref, normed_ref, xp_ref, we_ref, dw_ref, wp_ref, wqkv_ref, wo_ref, out_ref,
    outer, pad, rim, spatial, acc, grouped, proj, context, turn_ref, mask_ref,
):
    turn_ref[...] = turn_matrix()
    mask_ref[...] = head_mask()
    own = slice(1024 * part, 1024 * part + 1024)
    acc[...] = xp_ref[own].astype(F32)
    before, after = ((15, 8), (7, 0))[part]
    special = (before, after)[part]
    source = jnp.concatenate(
        [normed_ref[128 * special : 128 * special + 128], layer_norm(rim_ref[...].astype(F32))], axis=0
    )
    mixed_edge = mm(edge_matrix(part), source).astype(BF16)
    if part == 0:
        outer[0:128] = mixed_edge
        outer[128:256] = normed_ref[128 * after : 128 * after + 128]
    else:
        outer[0:128] = normed_ref[128 * before : 128 * before + 128]
        outer[128:256] = mixed_edge
    outer[256:304] = layer_norm(left_ref[...].astype(F32))
    outer[304:352] = layer_norm(right_ref[...].astype(F32))

    sub = lax.broadcasted_iota(jnp.int32, (8, CB), 0)

    def block(s, carry):
        for at in range(0, CB, 256):
            made = gelu(mm(normed_ref[own], we_ref[s, :, at : at + 256])).astype(BF16)
            pad[1:9, 1:9, :, at : at + 256] = made.reshape(8, 8, 16, 256)
            made = gelu(mm(outer[...], we_ref[s, :, at : at + 256])).astype(BF16)
            pad[0, 1:9, :, at : at + 256] = made[0:128].reshape(8, 16, 256)
            pad[9, 1:9, :, at : at + 256] = made[128:256].reshape(8, 16, 256)
            rim[:, at : at + 256] = made[256:352].astype(F32)
        for row in range(10):
            at = 8 * part + row
            last = pad[row, 8].astype(F32)
            first = pad[row, 1].astype(F32)
            west, east = [], []
            for b in range(2):
                turned = pltpu.roll(last[8 * b : 8 * b + 8], 1, 0)
                west.append(jnp.where(sub == 0, rim[at + 16 * b : at + 16 * b + 1], turned))
                turned = pltpu.roll(first[8 * b : 8 * b + 8], 7, 0)
                east.append(jnp.where(sub == 7, rim[at + 48 + 16 * b : at + 48 + 16 * b + 1], turned))
            pad[row, 0] = jnp.concatenate(west, axis=0).astype(BF16)
            pad[row, 9] = jnp.concatenate(east, axis=0).astype(BF16)

        taps = [[jnp.broadcast_to(dw_ref[s, a, b : b + 1].astype(BF16), (16, CB)) for b in range(3)] for a in range(3)]

        def pair_of_rows(pair, carry):
            for i in range(2):
                for j in range(8):
                    sums = [
                        pad[2 * pair + i + a, j] * taps[a][0]
                        + pad[2 * pair + i + a, j + 1] * taps[a][1]
                        + pad[2 * pair + i + a, j + 2] * taps[a][2]
                        for a in range(3)
                    ]
                    total = sums[0] + sums[1] + sums[2]
                    spatial[2 * pair + i, j] = gelu(total.astype(F32)).astype(BF16)
            rows = pl.ds(pl.multiple_of(256 * pair, 256), 256)
            acc[rows] += mm(spatial[pl.ds(2 * pair, 2)].reshape(256, CB), wp_ref[s])
            return carry

        lax.fori_loop(0, 4, pair_of_rows, 0, unroll=PAIRS)
        return carry

    lax.fori_loop(0, BLOCKS, block, 0)
    for pair in range(4):
        mixed = acc[256 * pair : 256 * pair + 256].astype(BF16)
        grouped[:, 16 * pair : 16 * pair + 16] = mm(turn_ref[...], mixed).astype(BF16).reshape(16, 16, CHANS)

    def emit(half, rows):
        rows = rows.reshape(4, 2, 8, 8, CHANS)
        for i in range(8):
            out_ref[i, :, half] = rows[:, :, i].reshape(4, 16, CHANS).astype(BF16)

    attention(grouped, wqkv_ref, wo_ref, mask_ref, proj, context, emit)


def local_part(part, rims, prepared):
    top, bottom, left, right = rims
    operands = ((top, bottom)[part], left, right, *prepared)
    return pl.pallas_call(
        functools.partial(local_kernel, part),
        in_specs=[in_vmem() for _ in operands],
        out_specs=in_vmem(),
        out_shape=jax.ShapeDtypeStruct((8, 4, 2, 16, CHANS), BF16),
        scratch_shapes=[
            pltpu.VMEM((352, CHANS), BF16),
            pltpu.VMEM((10, 10, 16, CB), BF16),
            pltpu.VMEM((96, CB), F32),
            pltpu.VMEM((8, 8, 16, CB), BF16),
            pltpu.VMEM((1024, CHANS), F32),
            *attention_scratch(),
        ],
        compiler_params=params(),
        cost_estimate=pl.CostEstimate(
            flops=4 * 1024 * CHANS * WIDE, bytes_accessed=8 * 2**20, transcendentals=2048 * WIDE
        ),
        name="local_part",
    )(*operands)


def exchange(blocks, groups):
    return lax.all_to_all(blocks, ("row", "col"), 0, 0, axis_index_groups=groups, tiled=True)


def on_device(field, w_expand, dw_kernel, w_project, qkv_block, out_block, qkv_grid, out_grid):
    n_row, n_col = lax.axis_size("row"), lax.axis_size("col")
    down = [(i, i + 1) for i in range(n_row - 1)]
    up = [(i + 1, i) for i in range(n_row - 1)]
    top = lax.ppermute(field[31], "row", down)
    bottom = lax.ppermute(field[0], "row", up)
    fill = jnp.zeros((14, CHANS), BF16)

    def rim(column):
        return jnp.concatenate([top[column : column + 1], field[:, column], bottom[column : column + 1], fill], axis=0)

    east, west = rim(63), rim(0)
    left = lax.ppermute(east, "col", [(i, i + 1) for i in range(n_col - 1)])
    right = lax.ppermute(west, "col", [(i + 1, i) for i in range(n_col - 1)])
    *prepared, qkv_block, out_block, qkv_grid, out_grid = prepare(
        east, field, w_expand, dw_kernel, w_project, qkv_block, out_block, qkv_grid, out_grid
    )
    groups = [[32 * row + 4 * j + c for row in range(n_row) for j in range(8)] for c in range(4)]
    gathered = []
    for part in range(2):
        blocked = local_part(part, (top, bottom, left, right), (*prepared, qkv_block, out_block))
        gathered.append(exchange(blocked.reshape(32, 2, 16, CHANS), groups).reshape(64, 16, CHANS))
    attended = grid_attention(gathered[0], qkv_grid, out_grid)
    attended = grid_attention(gathered[1], qkv_grid, out_grid, attended)
    home = exchange(attended, groups).reshape(8, 4, 2, 2, 16, CHANS)
    return home.transpose(3, 2, 0, 1, 4, 5).reshape(32, 64, CHANS)


def solution(mesh):
    placed = (P("row", "col", None), P(), P(), P(), P(), P(), P(), P())
    return jax.shard_map(
        on_device, mesh=mesh, in_specs=placed, out_specs=P("row", "col", None), check_vma=False
    )
```

profile of v0, /device:TPU:0, one launch (start us, length us, event | category | flops | bytes accessed | tf_op | source)
XLA Modules:
  0.0 146.6 jit_solution(608772945780544288)
XLA Ops:
  0.0 0.9 slice_bitcast_fusion
  0.9 1.3 collective-permute-start.1
  2.2 1.3 collective-permute-start
  3.5 1.1 fusion
  4.7 0.1 pad.7.clone
  4.7 0.0 collective-permute-done.1.rim_ref
  4.7 4.8 %collective-permute-done.rim_ref = bf16[64,512]{1,0:T(8,128)(2,1)S(1)} collective-permute-done((bf16[64,512]{1,0:T(8,128)(2,1)S(1)}, bf16[64,512]{1,0:T(8,128)(2,1)S(1)}, u32[]{:S(2)}, u32[]{:S(2)}) %collective-permute-start) | collective-permute-done | bytes 65568 | tf_op jit(solution)/shard_map/ppermute | solution.py:342
  9.5 0.1 maximum_maximum_fusion.1
  9.6 1.3 collective-permute-start.3
  10.9 4.5 %collective-permute-start.2 = (bf16[48,512]{1,0:T(8,128)(2,1)S(1)}, bf16[48,512]{1,0:T(8,128)(2,1)S(1)}, u32[]{:S(2)}, u32[]{:S(2)}) collective-permute-start(bf16[48,512]{1,0:T(8,128)(2,1)S(1)} %get-tuple-element.32.rest_4_), channel_id=1, source_target_pairs={{0,1},{1,2},{2,3},{3,4},{4,5},{5,6},{6,7},{7,8},{8,9},{9,10},{10,1... | collective-permute-start | bytes 147464 | tf_op jit(solution)/shard_map/ppermute | solution.py:349
  15.5 4.2 %prepare.1 = (bf16[2048,512]{1,0:T(8,128)(2,1)S(1)}, bf16[2048,512]{1,0:T(8,128)(2,1)S(1)}, bf16[2,512,1024]{2,1,0:T(8,128)(2,1)S(1)}, f32[2,3,3,1024]{3,2,1,0:T...) custom-call(bf16[2,16,64,512]{3,2,1,0:T(8,128)(2,1)} %bitcast.20, ...), custom_call_target="tpu_custom_call" | custom-call | flops 10000000000 | bytes 16777216 | tf_op jit(solution)/shard_map/prepare/pallas_call | solution.py:214
  19.7 0.0 copy-start
  19.7 1.2 copy-done
  20.8 0.0 copy-start.3
  20.8 0.0 copy-start.6
  20.8 0.0 copy-start.10
  20.8 0.0 copy-start.12
  20.9 0.0 copy-start.14
  20.9 0.0 collective-permute-done.3.right_ref
  20.9 0.0 collective-permute-done.2.left_ref
  20.9 15.7 %local_part.3 = bf16[8,4,2,16,512]{4,3,2,1,0:T(8,128)(2,1)} custom-call(bf16[64,512]{1,0:T(8,128)(2,1)S(1)} %collective-permute-done.1.rim_ref, bf16[48,512]{1,0:T(8,128)(2,1)S(1)} %collective-permute-done.2.left_ref, bf16[48,512]{1,0:T(8,128)(2,1)S(1)} %collective-permute-done.3.right_ref, bf16[2048,512]{1,0:T(8,128)(2,1)S(1)} %get-tuple-element.14.normed_ref, ...), custom_call_target="tpu_custom_call" | custom-call | flops 4294967296 | bytes 8388608 | tf_op jit(solution)/shard_map/local_part/pallas_call | solution.py:312
  36.6 0.0 copy-done.3
  36.6 0.0 copy-done.6
  36.6 0.0 copy-done.8
  36.6 0.0 copy-done.10
  36.6 0.0 copy-done.12
  36.6 0.0 copy-done.14
  36.6 12.6 %all-to-all-start.1 = ((bf16[32,2,16,512]{3,2,1,0:T(8,128)(2,1)}), bf16[32,2,16,512]{3,2,1,0:T(8,128)(2,1)S(1)}, u32[]{:S(2)}, u32[]{:S(2)}) async-start(bf16[32,2,16,512]{3,2,1,0:T(8,128)(2,1)} %bitcast.7), calls=%async_computation.1 | async-start | bytes 2097152 | tf_op jit(solution)/shard_map/all_to_all | solution.py:334
  49.3 0.0 copy-start.7
  49.3 1.6 %copy-done.7 = bf16[2048,512]{1,0:T(8,128)(2,1)S(1)} copy-done((bf16[2048,512]{1,0:T(8,128)(2,1)S(1)}, bf16[2048,512]{1,0:T(8,128)(2,1)}, u32[]{:S(2)}) %copy-start.7) | copy-done | bytes 2097176
  50.9 0.0 copy-start.9
  50.9 1.6 %copy-done.9 = bf16[2,512,1024]{2,1,0:T(8,128)(2,1)S(1)} copy-done((bf16[2,512,1024]{2,1,0:T(8,128)(2,1)S(1)}, bf16[2,512,1024]{2,1,0:T(8,128)(2,1)}, u32[]{:S(2)}) %copy-start.9) | copy-done | bytes 2097176
  52.5 1.6 %copy-done.11 = bf16[2,1024,512]{2,1,0:T(8,128)(2,1)S(1)} copy-done((bf16[2,1024,512]{2,1,0:T(8,128)(2,1)S(1)}, bf16[2,1024,512]{2,1,0:T(8,128)(2,1)}, u32[]{:S(2)}) %copy-start.11) | copy-done | bytes 2097176
  54.1 1.4 copy-done.13
  55.5 1.0 copy-done.15
  56.5 15.6 %local_part.2 = bf16[8,4,2,16,512]{4,3,2,1,0:T(8,128)(2,1)} custom-call(bf16[64,512]{1,0:T(8,128)(2,1)S(1)} %collective-permute-done.rim_ref, bf16[48,512]{1,0:T(8,128)(2,1)S(1)} %collective-permute-done.2.left_ref, bf16[48,512]{1,0:T(8,128)(2,1)S(1)} %collective-permute-done.3.right_ref, bf16[2048,512]{1,0:T(8,128)(2,1)S(1)} %get-tuple-element.14.normed_ref, ...), custom_call_target="tpu_custom_call" | custom-call | flops 4294967296 | bytes 8388608 | tf_op jit(solution)/shard_map/local_part/pallas_call | solution.py:312
  72.1 0.0 all-to-all-done.1
  72.1 10.0 %all-to-all-start = ((bf16[32,2,16,512]{3,2,1,0:T(8,128)(2,1)}), bf16[32,2,16,512]{3,2,1,0:T(8,128)(2,1)S(1)}, u32[]{:S(2)}, u32[]{:S(2)}) async-start(bf16[32,2,16,512]{3,2,1,0:T(8,128)(2,1)} %bitcast.5), calls=%async_computation | async-start | bytes 2097152 | tf_op jit(solution)/shard_map/all_to_all | solution.py:334
  82.1 0.0 copy-start.1
  82.2 1.4 copy-done.1
  83.6 1.0 copy-done.4
  84.6 6.3 %grid_attention.2.rest_0_ = bf16[32,2,16,512]{3,2,1,0:T(8,128)(2,1)S(1)} custom-call(bf16[64,16,512]{2,1,0:T(8,128)(2,1)S(1)} %bitcast.17, bf16[512,1536]{1,0:T(8,128)(2,1)S(1)} %copy-done.1, bf16[512,512]{1,0:T(8,128)(2,1)S(1)} %copy-done.4), custom_call_target="tpu_custom_call" | custom-call | flops 2147483648 | bytes 4194304 | tf_op jit(solution)/shard_map/grid_attention/pallas_call | solution.py:165
  90.9 11.0 %all-to-all-done = bf16[32,2,16,512]{3,2,1,0:T(8,128)(2,1)S(1)} async-done(((bf16[32,2,16,512]{3,2,1,0:T(8,128)(2,1)}), bf16[32,2,16,512]{3,2,1,0:T(8,128)(2,1)S(1)}, u32[]{:S(2)}, u32[]{:S(2)}) %all-to-all-start) | async-done | bytes 1048608 | tf_op jit(solution)/shard_map/all_to_all | solution.py:334
  102.0 1.4 copy-done.2
  103.4 1.0 copy-done.5
  104.4 6.3 %grid_attention.3 = bf16[32,2,2,16,512]{4,3,2,1,0:T(8,128)(2,1)S(1)} custom-call(bf16[64,16,512]{2,1,0:T(8,128)(2,1)S(1)} %bitcast.18, bf16[512,1536]{1,0:T(8,128)(2,1)S(1)} %copy-done.2, bf16[512,512]{1,0:T(8,128)(2,1)S(1)} %copy-done.5, bf16[32,2,16,512]{3,2,1,0:T(8,128)(2,1)S(1)} %grid_attention.2.rest_0_), custom_call_target="tpu_custom_call" | custom-call | flops 2147483648 | bytes 4194304 | tf_op jit(solution)/shard_map/grid_attention/pallas_call | solution.py:165
  110.7 34.3 %all_to_all.15 = bf16[32,2,2,16,512]{4,3,2,1,0:T(8,128)(2,1)S(1)} all-to-all(bf16[32,2,2,16,512]{4,3,2,1,0:T(8,128)(2,1)S(1)} %grid_attention.3), channel_id=1, replica_groups={{0,4,8,12,16,20,24,28,32,36,40,44,48,52,56,60,64,68,72,76,80,84,88,92,9..., dimensions={0} | all-to-all | bytes 4194304 | tf_op jit(solution)/shard_map/all_to_all | solution.py:334
  145.0 1.5 %copy.11 = bf16[2,2,8,4,16,512]{5,4,3,2,1,0:T(8,128)(2,1)} copy(bf16[2,2,8,4,16,512]{5,4,0,1,3,2:T(8,128)(2,1)S(1)} %bitcast.19) | data formatting | bytes 4194304 | tf_op jit(solution)/shard_map/transpose | solution.py:362
  (11 shorter events, 0.0 us)
Async XLA Ops:
  0.9 3.9 %collective-permute-start.1 = (bf16[64,512]{1,0:T(8,128)(2,1)S(1)}, bf16[64,512]{1,0:T(8,128)(2,1)S(1)}, u32[]{:S(2)}, u32[]{:S(2)}) collective-permute-start(bf16[64,512]{1,0:T(8,128)(2,1)S(1)} %get-tuple-element.25), channel_id=1, source_target_pairs={{0,32},{32,64},{64,96},{1,33},{33,65},{65,97},{2,34},{34,66},{66,9... | collective-permute-start | bytes 196616 | tf_op jit(solution)/shard_map/ppermute | solution.py:341
  2.2 7.3 %collective-permute-start = (bf16[64,512]{1,0:T(8,128)(2,1)S(1)}, bf16[64,512]{1,0:T(8,128)(2,1)S(1)}, u32[]{:S(2)}, u32[]{:S(2)}) collective-permute-start(bf16[64,512]{1,0:T(8,128)(2,1)S(1)} %get-tuple-element.26), channel_id=1, source_target_pairs={{32,0},{64,32},{96,64},{33,1},{65,33},{97,65},{34,2},{66,34},{98,6... | collective-permute-start | bytes 196616 | tf_op jit(solution)/shard_map/ppermute | solution.py:342
  9.6 11.2 %collective-permute-start.3 = (bf16[48,512]{1,0:T(8,128)(2,1)S(1)}, bf16[48,512]{1,0:T(8,128)(2,1)S(1)}, u32[]{:S(2)}, u32[]{:S(2)}) collective-permute-start(bf16[48,512]{1,0:T(8,128)(2,1)S(1)} %get-tuple-element.31), channel_id=1, source_target_pairs={{1,0},{2,1},{3,2},{4,3},{5,4},{6,5},{7,6},{8,7},{9,8},{10,9},{11,1... | collective-permute-start | bytes 147464 | tf_op jit(solution)/shard_map/ppermute | solution.py:350
  10.9 10.0 %collective-permute-start.2 = (bf16[48,512]{1,0:T(8,128)(2,1)S(1)}, bf16[48,512]{1,0:T(8,128)(2,1)S(1)}, u32[]{:S(2)}, u32[]{:S(2)}) collective-permute-start(bf16[48,512]{1,0:T(8,128)(2,1)S(1)} %get-tuple-element.32.rest_4_), channel_id=1, source_target_pairs={{0,1},{1,2},{2,3},{3,4},{4,5},{5,6},{6,7},{7,8},{8,9},{9,10},{10,1... | collective-permute-start | bytes 147464 | tf_op jit(solution)/shard_map/ppermute | solution.py:349
  19.7 1.2 copy-start
  20.8 15.8 %copy-start.3 = (bf16[512,512]{1,0:T(8,128)(2,1)}, bf16[512,512]{1,0:T(8,128)(2,1)S(1)}, u32[]{:S(2)}) copy-start(bf16[512,512]{1,0:T(8,128)(2,1)S(1)} %get-tuple-element.22.wo_ref) | copy-start | bytes 1572868
  20.8 15.8 %copy-start.6 = (bf16[2048,512]{1,0:T(8,128)(2,1)}, bf16[2048,512]{1,0:T(8,128)(2,1)S(1)}, u32[]{:S(2)}) copy-start(bf16[2048,512]{1,0:T(8,128)(2,1)S(1)} %get-tuple-element.15.xp_ref) | copy-start | bytes 6291460
  20.8 15.8 %copy-start.8 = (bf16[2,512,1024]{2,1,0:T(8,128)(2,1)}, bf16[2,512,1024]{2,1,0:T(8,128)(2,1)S(1)}, u32[]{:S(2)}) copy-start(bf16[2,512,1024]{2,1,0:T(8,128)(2,1)S(1)} %get-tuple-element.16.we_ref) | copy-start | bytes 6291460
  20.8 15.8 %copy-start.10 = (bf16[2,1024,512]{2,1,0:T(8,128)(2,1)}, bf16[2,1024,512]{2,1,0:T(8,128)(2,1)S(1)}, u32[]{:S(2)}) copy-start(bf16[2,1024,512]{2,1,0:T(8,128)(2,1)S(1)} %get-tuple-element.18.wp_ref) | copy-start | bytes 6291460
  20.8 15.8 %copy-start.12 = (bf16[512,1536]{1,0:T(8,128)(2,1)}, bf16[512,1536]{1,0:T(8,128)(2,1)S(1)}, u32[]{:S(2)}) copy-start(bf16[512,1536]{1,0:T(8,128)(2,1)S(1)} %get-tuple-element.19.wqkv_ref) | copy-start | bytes 4718596
  20.9 15.8 %copy-start.14 = (bf16[512,512]{1,0:T(8,128)(2,1)}, bf16[512,512]{1,0:T(8,128)(2,1)S(1)}, u32[]{:S(2)}) copy-start(bf16[512,512]{1,0:T(8,128)(2,1)S(1)} %get-tuple-element.20.wo_ref) | copy-start | bytes 1572868
  36.6 35.5 %all-to-all-start.1 = ((bf16[32,2,16,512]{3,2,1,0:T(8,128)(2,1)}), bf16[32,2,16,512]{3,2,1,0:T(8,128)(2,1)S(1)}, u32[]{:S(2)}, u32[]{:S(2)}) async-start(bf16[32,2,16,512]{3,2,1,0:T(8,128)(2,1)} %bitcast.7), calls=%async_computation.1 | async-start | bytes 2097152 | tf_op jit(solution)/shard_map/all_to_all | solution.py:334
  49.3 1.6 %copy-start.7 = (bf16[2048,512]{1,0:T(8,128)(2,1)S(1)}, bf16[2048,512]{1,0:T(8,128)(2,1)}, u32[]{:S(2)}) copy-start(bf16[2048,512]{1,0:T(8,128)(2,1)} %copy-done.6) | copy-start | bytes 6291460
  50.9 1.6 %copy-start.9 = (bf16[2,512,1024]{2,1,0:T(8,128)(2,1)S(1)}, bf16[2,512,1024]{2,1,0:T(8,128)(2,1)}, u32[]{:S(2)}) copy-start(bf16[2,512,1024]{2,1,0:T(8,128)(2,1)} %copy-done.8) | copy-start | bytes 6291460
  52.5 1.6 %copy-start.11 = (bf16[2,1024,512]{2,1,0:T(8,128)(2,1)S(1)}, bf16[2,1024,512]{2,1,0:T(8,128)(2,1)}, u32[]{:S(2)}) copy-start(bf16[2,1024,512]{2,1,0:T(8,128)(2,1)} %copy-done.10) | copy-start | bytes 6291460
  54.1 1.4 copy-start.13
  55.5 1.0 copy-start.15
  72.1 29.8 %all-to-all-start = ((bf16[32,2,16,512]{3,2,1,0:T(8,128)(2,1)}), bf16[32,2,16,512]{3,2,1,0:T(8,128)(2,1)S(1)}, u32[]{:S(2)}, u32[]{:S(2)}) async-start(bf16[32,2,16,512]{3,2,1,0:T(8,128)(2,1)} %bitcast.5), calls=%async_computation | async-start | bytes 2097152 | tf_op jit(solution)/shard_map/all_to_all | solution.py:334
  82.1 1.4 copy-start.1
  83.6 1.0 copy-start.4
  102.0 1.4 copy-start.2
  103.4 1.0 copy-start.5
where the time goes:
time: 148 us; the launch traced here: 147 us
  Pallas kernels  48.1 us (32%)
  blocking collectives  34.3 us (23%)
  starting transfers between devices  31.1 us (21%)
  local copies, waits for them, and re-layouts  16.9 us (11%)
  waiting for transfers between devices  15.8 us (11%)
    all_to_all x1, blocking collectives, exchange(): lax.all_to_all(blocks, ('row', 'col'), 0, 0, axis_index_groups=groups, ti...  34.3 us
    pallas_call x2, Pallas kernels, local_part(): pl.pallas_call(functools.partial(local_kernel, part), in_specs=[in_vmem()...  31.3 us
    all_to_all x2, starting transfers between devices, exchange(): lax.all_to_all(blocks, ('row', 'col'), 0, 0, axis_index_groups=groups, ti...  22.6 us
    unnamed x32, local copies, waits for them, and re-layouts  13.3 us
    pallas_call x2, Pallas kernels, grid_attention(): pl.pallas_call(grid_kernel, in_specs=[in_vmem() for _ in range(3 + len(ea...  12.6 us
    all_to_all x2, waiting for transfers between devices, exchange(): lax.all_to_all(blocks, ('row', 'col'), 0, 0, axis_index_groups=groups, ti...  11 us
    ppermute x1, waiting for transfers between devices, on_device(): bottom = lax.ppermute(field[0], 'row', up)  4.78 us
    ppermute x1, starting transfers between devices, on_device(): left = lax.ppermute(east, 'col', [(i, i + 1) for i in range(n_col - 1)])  4.55 us
  transfers between devices with their start and end apart: 6, of which 2 were waited for; matrix products, arithmetic and copies ran while one was open for 1% of the time, Pallas kernels for 18%

commit v1 on v0

--- a/solution.py
+++ b/solution.py
@@ -16,7 +16,8 @@
 CB = 1024
 BLOCKS = WIDE // CB
 PAIRS = 4
-VMEM_LIMIT = 28 * 2**20
+PIECES = CB // 256
+VMEM_LIMIT = 36 * 2**20
 SCALE_LOG2 = float(HEAD**-0.5 * np.log2(np.e))
 
 
@@ -127,8 +128,9 @@
     lax.fori_loop(0, 2, one, 0, unroll=2)
 
 
-def grid_kernel(x_ref, wqkv_ref, wo_ref, *rest):
-    out_ref, grouped, proj, context, turn_ref, mask_ref = rest[-6:]
+def grid_kernel(x_ref, wqkv_hbm, wo_hbm, *rest):
+    out_ref, grouped, proj, context, turn_ref, mask_ref, wqkv_ref, wo_ref, sems = rest[-9:]
+    copies = fetch(sems, (wqkv_hbm, wqkv_ref), (wo_hbm, wo_ref))
     turn_ref[...] = turn_matrix()
     mask_ref[...] = head_mask()
     for t in range(4):
@@ -138,15 +140,17 @@
     def emit(half, rows):
         grouped[pl.ds(8 * half, 8)] = rows.astype(BF16).reshape(8, 64, CHANS)
 
+    for copy in copies:
+        copy.wait()
     attention(grouped, wqkv_ref, wo_ref, mask_ref, proj, context, emit)
     for t in range(4):
         moved = mm(turn_ref[...], grouped[:, 16 * t : 16 * t + 16].reshape(256, CHANS))
         moved = moved.astype(BF16).reshape(8, 2, 16, CHANS)
-        if len(rest) == 6:
+        if len(rest) == 9:
             out_ref[8 * t : 8 * t + 8] = moved
         else:
             out_ref[8 * t : 8 * t + 8, 1] = moved
-    if len(rest) > 6:
+    if len(rest) > 9:
         out_ref[:, 0] = rest[0][...]
 
 
@@ -157,6 +161,8 @@
         pltpu.VMEM((512, CHANS), BF16),
         pltpu.VMEM((256, 256), BF16),
         pltpu.VMEM((256, 128), BF16),
+        pltpu.VMEM((CHANS, 3 * CHANS), BF16),
+        pltpu.VMEM((CHANS, CHANS), BF16),
     ]
 
 
@@ -164,99 +170,94 @@
     shape = (32, 2, 2, 16, CHANS) if earlier else (32, 2, 16, CHANS)
     return pl.pallas_call(
         grid_kernel,
-        in_specs=[in_vmem() for _ in range(3 + len(earlier))],
+        in_specs=[in_vmem(), *in_hbm(2), *[in_vmem() for _ in earlier]],
         out_specs=in_vmem(),
         out_shape=jax.ShapeDtypeStruct(shape, BF16),
-        scratch_shapes=attention_scratch(),
+        scratch_shapes=[*attention_scratch(), pltpu.SemaphoreType.DMA((2,))],
         compiler_params=params(),
         cost_estimate=pl.CostEstimate(
             flops=8 * 1024 * CHANS * CHANS, bytes_accessed=4 * 2**20, transcendentals=2**20
         ),
         name="grid_attention",
-    )(x, qkv, out_proj, *earlier)
-
-
-def prepare_kernel(x_hbm, we_hbm, dw_hbm, wp_hbm, *rest):
-    small_hbm, (_, normed_ref, xp_ref, we_ref, dw_ref, wp_ref), small, (x_ref, spread_ref, sems) = (
-        rest[0:4], rest[4:10], rest[10:14], rest[14:],
-    )
-    rows = [
-        fetch(sems.at[0, pl.ds(k, 1)], (x_hbm.at[:, 8 * k : 8 * k + 8], x_ref.at[:, 8 * k : 8 * k + 8]))[0]
-        for k in range(2)
-    ]
-    copies = fetch(
-        sems.at[1],
-        *[(we_hbm.at[:, CB * s : CB * s + CB], we_ref.at[s]) for s in range(BLOCKS)],
-        *[(dw_hbm.at[:, :, CB * s : CB * s + CB], dw_ref.at[s]) for s in range(BLOCKS)],
-        *[(wp_hbm.at[CB * s : CB * s + CB], wp_ref.at[s]) for s in range(BLOCKS)],
-        *zip(small_hbm, small),
-    )
-    spread_ref[...] = spread_matrix()
-    for pair in range(8):
-        if pair % 4 == 0:
-            rows[pair // 4].wait()
-        moved = mm(spread_ref[...], x_ref[:, 2 * pair : 2 * pair + 2].reshape(256, CHANS))
+    )(x, *kept_in_hbm(qkv, out_proj), *earlier)
+
+
+def prepare_kernel(x_ref, _, normed_ref, xp_ref):
+    spread = spread_matrix()
+    for pair in range(4):
+        moved = mm(spread, x_ref[:, 2 * pair : 2 * pair + 2].reshape(256, CHANS))
         xp_ref[256 * pair : 256 * pair + 256] = moved.astype(BF16)
         normed_ref[256 * pair : 256 * pair + 256] = layer_norm(moved)
-    for copy in copies:
-        copy.wait()
-
-
-def prepare(after, field, w_expand, dw_kernel, w_project, *small):
-    out_shape = [
-        jax.ShapeDtypeStruct((2048, CHANS), BF16),
-        jax.ShapeDtypeStruct((2048, CHANS), BF16),
-        jax.ShapeDtypeStruct((BLOCKS, CHANS, CB), BF16),
-        jax.ShapeDtypeStruct((BLOCKS, 3, 3, CB), F32),
-        jax.ShapeDtypeStruct((BLOCKS, CB, CHANS), BF16),
-        *[jax.ShapeDtypeStruct(a.shape, BF16) for a in small],
-    ]
+
+
+def prepare(field, after):
     return pl.pallas_call(
         prepare_kernel,
-        in_specs=[*in_hbm(8), pl.BlockSpec(memory_space=pl.ANY)],
-        out_specs=[in_vmem() for _ in out_shape],
-        out_shape=out_shape,
-        scratch_shapes=[
-            pltpu.VMEM((2, 16, 64, CHANS), BF16),
-            pltpu.VMEM((256, 256), BF16),
-            pltpu.SemaphoreType.DMA((2, 4 + 3 * BLOCKS)),
+        grid=(2,),
+        in_specs=[
+            pl.BlockSpec((2, 8, 64, CHANS), lambda k: (0, k, 0, 0)),
+            pl.BlockSpec(memory_space=pl.ANY),
         ],
+        out_specs=[pl.BlockSpec((1024, CHANS), lambda k: (k, 0))] * 2,
+        out_shape=[pltpu.HBM((2048, CHANS), BF16)] * 2,
         compiler_params=params(),
         cost_estimate=pl.CostEstimate(flops=10**10, bytes_accessed=16 * 2**20, transcendentals=0),
         name="prepare",
-    )(*kept_in_hbm(field.reshape(2, 16, 64, CHANS), w_expand, dw_kernel, w_project, *small), after)
+    )(kept_in_hbm(field.reshape(2, 16, 64, CHANS))[0], after)
 
 
 def local_kernel(
-    part, rim_ref, left_ref, right_ref, normed_ref, xp_ref, we_ref, dw_ref, wp_ref, wqkv_ref, wo_ref, out_ref,
-    outer, pad, rim, spatial, acc, grouped, proj, context, turn_ref, mask_ref,
+    part, rim_ref, left_ref, right_ref, normed_hbm, xp_hbm, we_hbm, dw_hbm, wp_hbm, wqkv_hbm, wo_hbm, out_ref,
+    normed_ref, outer, special_ref, xp_ref, we_ref, dw_ref, wp_ref, pad, rim, spatial, acc,
+    grouped, proj, context, turn_ref, mask_ref, wqkv_ref, wo_ref, sems,
 ):
+    before, after = ((15, 8), (7, 0))[part]
+    special, plain = ((before, after), (after, before))[part]
+    plain_at = (128, 0)[part]
+    first = fetch(
+        sems.at[0],
+        (normed_hbm.at[128 * special : 128 * special + 128], special_ref),
+        (normed_hbm.at[1024 * part : 1024 * part + 1024], normed_ref),
+        (normed_hbm.at[128 * plain : 128 * plain + 128], outer.at[plain_at : plain_at + 128]),
+    )
+
+    def expansion(s, piece):
+        lanes = pl.ds(pl.multiple_of(CB * s + 256 * piece, 256), 256)
+        return pltpu.make_async_copy(we_hbm.at[:, lanes], we_ref.at[s, piece], sems.at[1 + s, piece])
+
+    def others(s):
+        lanes = pl.ds(pl.multiple_of(CB * s, CB), CB)
+        return [
+            pltpu.make_async_copy(dw_hbm.at[:, :, lanes], dw_ref.at[s], sems.at[1 + s, PIECES]),
+            pltpu.make_async_copy(wp_hbm.at[lanes], wp_ref.at[s], sems.at[1 + s, PIECES + 1]),
+        ]
+
+    for s in range(BLOCKS):
+        for piece in range(PIECES):
+            expansion(s, piece).start()
+        for copy in others(s):
+            copy.start()
+    last = fetch(sems.at[1 + BLOCKS], (xp_hbm.at[1024 * part : 1024 * part + 1024], xp_ref), (wqkv_hbm, wqkv_ref), (wo_hbm, wo_ref))
     turn_ref[...] = turn_matrix()
     mask_ref[...] = head_mask()
-    own = slice(1024 * part, 1024 * part + 1024)
-    acc[...] = xp_ref[own].astype(F32)
-    before, after = ((15, 8), (7, 0))[part]
-    special = (before, after)[part]
-    source = jnp.concatenate(
-        [normed_ref[128 * special : 128 * special + 128], layer_norm(rim_ref[...].astype(F32))], axis=0
-    )
-    mixed_edge = mm(edge_matrix(part), source).astype(BF16)
-    if part == 0:
-        outer[0:128] = mixed_edge
-        outer[128:256] = normed_ref[128 * after : 128 * after + 128]
-    else:
-        outer[0:128] = normed_ref[128 * before : 128 * before + 128]
-        outer[128:256] = mixed_edge
     outer[256:304] = layer_norm(left_ref[...].astype(F32))
     outer[304:352] = layer_norm(right_ref[...].astype(F32))
+    acc[...] = jnp.zeros_like(acc)
+    first[0].wait()
+    source = jnp.concatenate([special_ref[...], layer_norm(rim_ref[...].astype(F32))], axis=0)
+    outer[128 - plain_at : 256 - plain_at] = mm(edge_matrix(part), source).astype(BF16)
+    for copy in first[1:]:
+        copy.wait()
 
     sub = lax.broadcasted_iota(jnp.int32, (8, CB), 0)
 
     def block(s, carry):
-        for at in range(0, CB, 256):
-            made = gelu(mm(normed_ref[own], we_ref[s, :, at : at + 256])).astype(BF16)
+        for piece in range(PIECES):
+            at = 256 * piece
+            expansion(s, piece).wait()
+            made = gelu(mm(normed_ref[...], we_ref[s, piece])).astype(BF16)
             pad[1:9, 1:9, :, at : at + 256] = made.reshape(8, 8, 16, 256)
-            made = gelu(mm(outer[...], we_ref[s, :, at : at + 256])).astype(BF16)
+            made = gelu(mm(outer[...], we_ref[s, piece])).astype(BF16)
             pad[0, 1:9, :, at : at + 256] = made[0:128].reshape(8, 16, 256)
             pad[9, 1:9, :, at : at + 256] = made[128:256].reshape(8, 16, 256)
             rim[:, at : at + 256] = made[256:352].astype(F32)
@@ -273,6 +274,8 @@
             pad[row, 0] = jnp.concatenate(west, axis=0).astype(BF16)
             pad[row, 9] = jnp.concatenate(east, axis=0).astype(BF16)
 
+        for copy in others(s):
+            copy.wait()
         taps = [[jnp.broadcast_to(dw_ref[s, a, b : b + 1].astype(BF16), (16, CB)) for b in range(3)] for a in range(3)]
 
         def pair_of_rows(pair, carry):
@@ -294,8 +297,11 @@
         return carry
 
     lax.fori_loop(0, BLOCKS, block, 0)
+    for copy in last:
+        copy.wait()
     for pair in range(4):
-        mixed = acc[256 * pair : 256 * pair + 256].astype(BF16)
+        rows = slice(256 * pair, 256 * pair + 256)
+        mixed = (xp_ref[rows].astype(F32) + acc[rows]).astype(BF16)
         grouped[:, 16 * pair : 16 * pair + 16] = mm(turn_ref[...], mixed).astype(BF16).reshape(16, 16, CHANS)
 
     def emit(half, rows):
@@ -306,28 +312,34 @@
     attention(grouped, wqkv_ref, wo_ref, mask_ref, proj, context, emit)
 
 
-def local_part(part, rims, prepared):
+def local_part(part, rims, *arrays):
     top, bottom, left, right = rims
-    operands = ((top, bottom)[part], left, right, *prepared)
     return pl.pallas_call(
         functools.partial(local_kernel, part),
-        in_specs=[in_vmem() for _ in operands],
+        in_specs=[*[in_vmem() for _ in range(3)], *in_hbm(len(arrays))],
         out_specs=in_vmem(),
         out_shape=jax.ShapeDtypeStruct((8, 4, 2, 16, CHANS), BF16),
         scratch_shapes=[
+            pltpu.VMEM((1024, CHANS), BF16),
             pltpu.VMEM((352, CHANS), BF16),
+            pltpu.VMEM((128, CHANS), BF16),
+            pltpu.VMEM((1024, CHANS), BF16),
+            pltpu.VMEM((BLOCKS, PIECES, CHANS, 256), BF16),
+            pltpu.VMEM((BLOCKS, 3, 3, CB), F32),
+            pltpu.VMEM((BLOCKS, CB, CHANS), BF16),
             pltpu.VMEM((10, 10, 16, CB), BF16),
             pltpu.VMEM((96, CB), F32),
             pltpu.VMEM((8, 8, 16, CB), BF16),
             pltpu.VMEM((1024, CHANS), F32),
             *attention_scratch(),
+            pltpu.SemaphoreType.DMA((2 + BLOCKS, PIECES + 2)),
         ],
         compiler_params=params(),
         cost_estimate=pl.CostEstimate(
             flops=4 * 1024 * CHANS * WIDE, bytes_accessed=8 * 2**20, transcendentals=2048 * WIDE
         ),
         name="local_part",
-    )(*operands)
+    )((top, bottom)[part], left, right, *kept_in_hbm(*arrays))
 
 
 def exchange(blocks, groups):
@@ -348,13 +360,13 @@
     east, west = rim(63), rim(0)
     left = lax.ppermute(east, "col", [(i, i + 1) for i in range(n_col - 1)])
     right = lax.ppermute(west, "col", [(i + 1, i) for i in range(n_col - 1)])
-    *prepared, qkv_block, out_block, qkv_grid, out_grid = prepare(
-        east, field, w_expand, dw_kernel, w_project, qkv_block, out_block, qkv_grid, out_grid
-    )
+    normed, xp = prepare(field, east)
     groups = [[32 * row + 4 * j + c for row in range(n_row) for j in range(8)] for c in range(4)]
     gathered = []
     for part in range(2):
-        blocked = local_part(part, (top, bottom, left, right), (*prepared, qkv_block, out_block))
+        blocked = local_part(
+            part, (top, bottom, left, right), normed, xp, w_expand, dw_kernel, w_project, qkv_block, out_block
+        )
         gathered.append(exchange(blocked.reshape(32, 2, 16, CHANS), groups).reshape(64, 16, CHANS))
     attended = grid_attention(gathered[0], qkv_grid, out_grid)
     attended = grid_attention(gathered[1], qkv_grid, out_grid, attended)

time: 148 us -> 146 us (0.986)
  local copies, waits for them, and re-layouts: 16.9 us -> 3.64 us
  Pallas kernels: 48.1 us -> 57.6 us
  waiting for transfers between devices: 15.8 us -> 17.8 us
    unnamed x32 -> x0, local copies, waits for them, and re-layouts: 13.3 us -> none
    pallas_call x5, Pallas kernels: 48.1 us -> 57.6 us  [the longest x2 38.2 us: local_part(): pl.pallas_call(functools.partial(local_kernel, part), in_specs=[*[in_vmem...]
    all_to_all x2, waiting for transfers between devices: 11 us -> 13 us  [exchange(): lax.all_to_all(blocks, ('row', 'col'), 0, 0, axis_index_groups=groups, ti...]
  transfers between devices with their start and end apart: 6 -> 6, of which waited for: 2 -> 3; matrix products, arithmetic and copies ran while one was open for 1% -> 1% of each run, Pallas kernels for 18% -> 21%
where the time goes in v1:
time: 146 us; the launch traced here: 145 us
  Pallas kernels  57.6 us (39%)
  blocking collectives  34.3 us (23%)
  starting transfers between devices  31.5 us (22%)
  waiting for transfers between devices  17.8 us (12%)
  local copies, waits for them, and re-layouts  3.64 us (2%)
    pallas_call x2, Pallas kernels, local_part(): pl.pallas_call(functools.partial(local_kernel, part), in_specs=[*[in_vmem...  38.2 us
    all_to_all x1, blocking collectives, exchange(): lax.all_to_all(blocks, ('row', 'col'), 0, 0, axis_index_groups=groups, ti...  34.3 us
    all_to_all x2, starting transfers between devices, exchange(): lax.all_to_all(blocks, ('row', 'col'), 0, 0, axis_index_groups=groups, ti...  23.1 us
    pallas_call x2, Pallas kernels, grid_attention(): pl.pallas_call(grid_kernel, in_specs=[in_vmem(), *in_hbm(2), *[in_vmem()...  15.5 us
    all_to_all x2, waiting for transfers between devices, exchange(): lax.all_to_all(blocks, ('row', 'col'), 0, 0, axis_index_groups=groups, ti...  13 us
    ppermute x1, waiting for transfers between devices, on_device(): bottom = lax.ppermute(field[0], 'row', up)  4.78 us
    ppermute x1, starting transfers between devices, on_device(): left = lax.ppermute(east, 'col', [(i, i + 1) for i in range(n_col - 1)])  4.55 us
    pallas_call x1, Pallas kernels, prepare(): pl.pallas_call(prepare_kernel, grid=(2,), in_specs=[pl.BlockSpec((2, 8, 6...  3.9 us
  transfers between devices with their start and end apart: 6, of which 3 were waited for; matrix products, arithmetic and copies ran while one was open for 1% of the time, Pallas kernels for 21%

profile of v1, /device:TPU:0, one launch (start us, length us, event | category | flops | bytes accessed | tf_op | source)
XLA Modules:
  0.0 145.0 jit_solution(17212555673946888192)
XLA Ops:
  0.0 0.9 slice_bitcast_fusion
  0.9 1.3 collective-permute-start.1
  2.2 1.3 collective-permute-start
  3.5 1.1 fusion
  4.7 0.1 pad.7.clone
  4.7 0.0 collective-permute-done.1.rim_ref
  4.7 4.8 %collective-permute-done.rim_ref = bf16[64,512]{1,0:T(8,128)(2,1)S(1)} collective-permute-done((bf16[64,512]{1,0:T(8,128)(2,1)S(1)}, bf16[64,512]{1,0:T(8,128)(2,1)S(1)}, u32[]{:S(2)}, u32[]{:S(2)}) %collective-permute-start) | collective-permute-done | bytes 65568 | tf_op jit(solution)/shard_map/ppermute | solution.py:354
  9.5 0.1 maximum_maximum_fusion.1
  9.6 1.3 collective-permute-start.3
  10.9 4.5 %collective-permute-start.2 = (bf16[48,512]{1,0:T(8,128)(2,1)S(1)}, bf16[48,512]{1,0:T(8,128)(2,1)S(1)}, u32[]{:S(2)}, u32[]{:S(2)}) collective-permute-start(bf16[48,512]{1,0:T(8,128)(2,1)S(1)} %get-tuple-element.18._), channel_id=1, source_target_pairs={{0,1},{1,2},{2,3},{3,4},{4,5},{5,6},{6,7},{7,8},{8,9},{9,10},{10,1... | collective-permute-start | bytes 147464 | tf_op jit(solution)/shard_map/ppermute | solution.py:361
  15.5 3.9 %prepare.1 = (bf16[2048,512]{1,0:T(8,128)(2,1)}, bf16[2048,512]{1,0:T(8,128)(2,1)}) custom-call(bf16[2,16,64,512]{3,2,1,0:T(8,128)(2,1)} %bitcast.20, bf16[48,512]{1,0:T(8,128)(2,1)S(1)} %get-tuple-element.18._), custom_call_target="tpu_custom_call" | custom-call | flops 10000000000 | bytes 16777216 | tf_op jit(solution)/shard_map/prepare/pallas_call | solution.py:194
  19.4 0.0 collective-permute-done.3.right_ref
  19.4 0.0 collective-permute-done.2.left_ref
  19.4 19.1 %local_part.3 = bf16[8,4,2,16,512]{4,3,2,1,0:T(8,128)(2,1)} custom-call(bf16[64,512]{1,0:T(8,128)(2,1)S(1)} %collective-permute-done.1.rim_ref, bf16[48,512]{1,0:T(8,128)(2,1)S(1)} %collective-permute-done.2.left_ref, bf16[48,512]{1,0:T(8,128)(2,1)S(1)} %collective-permute-done.3.right_ref, bf16[2048,512]{1,0:T(8,128)(2,1)} %get-tuple-element.7.normed_hbm, ...), custom_call_target="tpu_custom_call" | custom-call | flops 4294967296 | bytes 8388608 | tf_op jit(solution)/shard_map/local_part/pallas_call | solution.py:317
  38.5 14.0 %all-to-all-start.1 = ((bf16[32,2,16,512]{3,2,1,0:T(8,128)(2,1)}), bf16[32,2,16,512]{3,2,1,0:T(8,128)(2,1)S(1)}, u32[]{:S(2)}, u32[]{:S(2)}) async-start(bf16[32,2,16,512]{3,2,1,0:T(8,128)(2,1)} %bitcast.7), calls=%async_computation.1 | async-start | bytes 2097152 | tf_op jit(solution)/shard_map/all_to_all | solution.py:346
  52.5 19.1 %local_part.2 = bf16[8,4,2,16,512]{4,3,2,1,0:T(8,128)(2,1)} custom-call(bf16[64,512]{1,0:T(8,128)(2,1)S(1)} %collective-permute-done.rim_ref, bf16[48,512]{1,0:T(8,128)(2,1)S(1)} %collective-permute-done.2.left_ref, bf16[48,512]{1,0:T(8,128)(2,1)S(1)} %collective-permute-done.3.right_ref, bf16[2048,512]{1,0:T(8,128)(2,1)} %get-tuple-element.7.normed_hbm, ...), custom_call_target="tpu_custom_call" | custom-call | flops 4294967296 | bytes 8388608 | tf_op jit(solution)/shard_map/local_part/pallas_call | solution.py:317
  71.6 0.9 all-to-all-done.1
  72.5 9.1 %all-to-all-start = ((bf16[32,2,16,512]{3,2,1,0:T(8,128)(2,1)}), bf16[32,2,16,512]{3,2,1,0:T(8,128)(2,1)S(1)}, u32[]{:S(2)}, u32[]{:S(2)}) async-start(bf16[32,2,16,512]{3,2,1,0:T(8,128)(2,1)} %bitcast.5), calls=%async_computation | async-start | bytes 2097152 | tf_op jit(solution)/shard_map/all_to_all | solution.py:346
  81.6 7.7 %grid_attention.2.rest_0_ = bf16[32,2,16,512]{3,2,1,0:T(8,128)(2,1)S(1)} custom-call(bf16[64,16,512]{2,1,0:T(8,128)(2,1)S(1)} %bitcast.17, bf16[512,1536]{1,0:T(8,128)(2,1)} %wqkv_hbm.7, bf16[512,512]{1,0:T(8,128)(2,1)} %wo_hbm.7), custom_call_target="tpu_custom_call" | custom-call | flops 2147483648 | bytes 4194304 | tf_op jit(solution)/shard_map/grid_attention/pallas_call | solution.py:171
  89.4 12.1 %all-to-all-done = bf16[32,2,16,512]{3,2,1,0:T(8,128)(2,1)S(1)} async-done(((bf16[32,2,16,512]{3,2,1,0:T(8,128)(2,1)}), bf16[32,2,16,512]{3,2,1,0:T(8,128)(2,1)S(1)}, u32[]{:S(2)}, u32[]{:S(2)}) %all-to-all-start) | async-done | bytes 1048608 | tf_op jit(solution)/shard_map/all_to_all | solution.py:346
  101.4 7.7 %grid_attention.3 = bf16[32,2,2,16,512]{4,3,2,1,0:T(8,128)(2,1)S(1)} custom-call(bf16[64,16,512]{2,1,0:T(8,128)(2,1)S(1)} %bitcast.18, bf16[512,1536]{1,0:T(8,128)(2,1)} %wqkv_hbm.7, bf16[512,512]{1,0:T(8,128)(2,1)} %wo_hbm.7, bf16[32,2,16,512]{3,2,1,0:T(8,128)(2,1)S(1)} %grid_attention.2.rest_0_), custom_call_target="tpu_custom_call" | custom-call | flops 2147483648 | bytes 4194304 | tf_op jit(solution)/shard_map/grid_attention/pallas_call | solution.py:171
  109.2 34.3 %all_to_all.15 = bf16[32,2,2,16,512]{4,3,2,1,0:T(8,128)(2,1)S(1)} all-to-all(bf16[32,2,2,16,512]{4,3,2,1,0:T(8,128)(2,1)S(1)} %grid_attention.3), channel_id=1, replica_groups={{0,4,8,12,16,20,24,28,32,36,40,44,48,52,56,60,64,68,72,76,80,84,88,92,9..., dimensions={0} | all-to-all | bytes 4194304 | tf_op jit(solution)/shard_map/all_to_all | solution.py:346
  143.5 1.5 %copy.11 = bf16[2,2,8,4,16,512]{5,4,3,2,1,0:T(8,128)(2,1)} copy(bf16[2,2,8,4,16,512]{5,4,0,1,3,2:T(8,128)(2,1)S(1)} %bitcast.19) | data formatting | bytes 4194304 | tf_op jit(solution)/shard_map/transpose | solution.py:374
  (4 shorter events, 0.0 us)
Async XLA Ops:
  0.9 3.9 %collective-permute-start.1 = (bf16[64,512]{1,0:T(8,128)(2,1)S(1)}, bf16[64,512]{1,0:T(8,128)(2,1)S(1)}, u32[]{:S(2)}, u32[]{:S(2)}) collective-permute-start(bf16[64,512]{1,0:T(8,128)(2,1)S(1)} %get-tuple-element.11), channel_id=1, source_target_pairs={{0,32},{32,64},{64,96},{1,33},{33,65},{65,97},{2,34},{34,66},{66,9... | collective-permute-start | bytes 196616 | tf_op jit(solution)/shard_map/ppermute | solution.py:353
  2.2 7.3 %collective-permute-start = (bf16[64,512]{1,0:T(8,128)(2,1)S(1)}, bf16[64,512]{1,0:T(8,128)(2,1)S(1)}, u32[]{:S(2)}, u32[]{:S(2)}) collective-permute-start(bf16[64,512]{1,0:T(8,128)(2,1)S(1)} %get-tuple-element.12), channel_id=1, source_target_pairs={{32,0},{64,32},{96,64},{33,1},{65,33},{97,65},{34,2},{66,34},{98,6... | collective-permute-start | bytes 196616 | tf_op jit(solution)/shard_map/ppermute | solution.py:354
  9.6 9.8 %collective-permute-start.3 = (bf16[48,512]{1,0:T(8,128)(2,1)S(1)}, bf16[48,512]{1,0:T(8,128)(2,1)S(1)}, u32[]{:S(2)}, u32[]{:S(2)}) collective-permute-start(bf16[48,512]{1,0:T(8,128)(2,1)S(1)} %get-tuple-element.17), channel_id=1, source_target_pairs={{1,0},{2,1},{3,2},{4,3},{5,4},{6,5},{7,6},{8,7},{9,8},{10,9},{11,1... | collective-permute-start | bytes 147464 | tf_op jit(solution)/shard_map/ppermute | solution.py:362
  10.9 8.5 %collective-permute-start.2 = (bf16[48,512]{1,0:T(8,128)(2,1)S(1)}, bf16[48,512]{1,0:T(8,128)(2,1)S(1)}, u32[]{:S(2)}, u32[]{:S(2)}) collective-permute-start(bf16[48,512]{1,0:T(8,128)(2,1)S(1)} %get-tuple-element.18._), channel_id=1, source_target_pairs={{0,1},{1,2},{2,3},{3,4},{4,5},{5,6},{6,7},{7,8},{8,9},{9,10},{10,1... | collective-permute-start | bytes 147464 | tf_op jit(solution)/shard_map/ppermute | solution.py:361
  38.5 34.0 %all-to-all-start.1 = ((bf16[32,2,16,512]{3,2,1,0:T(8,128)(2,1)}), bf16[32,2,16,512]{3,2,1,0:T(8,128)(2,1)S(1)}, u32[]{:S(2)}, u32[]{:S(2)}) async-start(bf16[32,2,16,512]{3,2,1,0:T(8,128)(2,1)} %bitcast.7), calls=%async_computation.1 | async-start | bytes 2097152 | tf_op jit(solution)/shard_map/all_to_all | solution.py:346
  72.5 28.9 %all-to-all-start = ((bf16[32,2,16,512]{3,2,1,0:T(8,128)(2,1)}), bf16[32,2,16,512]{3,2,1,0:T(8,128)(2,1)S(1)}, u32[]{:S(2)}, u32[]{:S(2)}) async-start(bf16[32,2,16,512]{3,2,1,0:T(8,128)(2,1)} %bitcast.5), calls=%async_computation | async-start | bytes 2097152 | tf_op jit(solution)/shard_map/all_to_all | solution.py:346

commit v2 on v1

--- a/solution.py
+++ b/solution.py
@@ -106,12 +106,22 @@
     return jnp.concatenate(found, axis=1)
 
 
-def attention(grouped, wqkv_ref, wo_ref, mask_ref, proj, context, emit):
+def weight_fetches(wqkv_hbm, wo_hbm, wqkv_ref, wo_ref, sems):
+    copies = [
+        pltpu.make_async_copy(wqkv_hbm.at[:, CHANS * k : CHANS * k + CHANS], wqkv_ref.at[k], sems.at[k]) for k in range(3)
+    ]
+    return [*copies, pltpu.make_async_copy(wo_hbm, wo_ref, sems.at[3])]
+
+
+def attention(grouped, wqkv_ref, wo_ref, mask_ref, proj, context, copies, emit):
     mask = mask_ref[...]
-
-    def one(half, carry):
-        x = grouped[pl.ds(8 * half, 8)].reshape(512, CHANS).astype(F32)
-        proj[...] = mm(layer_norm(x), wqkv_ref[...]).astype(BF16)
+    for half in range(2):
+        x = grouped[8 * half : 8 * half + 8].reshape(512, CHANS).astype(F32)
+        normed = layer_norm(x)
+        for k in range(3):
+            if half == 0:
+                copies[k].wait()
+            proj[:, CHANS * k : CHANS * k + CHANS] = mm(normed, wqkv_ref[k]).astype(BF16)
         for g in range(8):
             rows = slice(64 * g, 64 * g + 64)
             for at in range(0, CHANS, 128):
@@ -122,15 +132,16 @@
                 weights = jnp.exp2((scores - segment_max(scores)) * SCALE_LOG2).astype(BF16)
                 both = mm(weights, jnp.concatenate([values, mask], axis=1))
                 context[rows, at : at + 128] = (both[:, :128] / both[:, 128:]).astype(BF16)
+        if half == 0:
+            copies[3].wait()
         emit(half, x + mm(context[...], wo_ref[...]))
-        return carry
-
-    lax.fori_loop(0, 2, one, 0, unroll=2)
 
 
 def grid_kernel(x_ref, wqkv_hbm, wo_hbm, *rest):
     out_ref, grouped, proj, context, turn_ref, mask_ref, wqkv_ref, wo_ref, sems = rest[-9:]
-    copies = fetch(sems, (wqkv_hbm, wqkv_ref), (wo_hbm, wo_ref))
+    copies = weight_fetches(wqkv_hbm, wo_hbm, wqkv_ref, wo_ref, sems)
+    for copy in copies:
+        copy.start()
     turn_ref[...] = turn_matrix()
     mask_ref[...] = head_mask()
     for t in range(4):
@@ -140,9 +151,7 @@
     def emit(half, rows):
         grouped[pl.ds(8 * half, 8)] = rows.astype(BF16).reshape(8, 64, CHANS)
 
-    for copy in copies:
-        copy.wait()
-    attention(grouped, wqkv_ref, wo_ref, mask_ref, proj, context, emit)
+    attention(grouped, wqkv_ref, wo_ref, mask_ref, proj, context, copies, emit)
     for t in range(4):
         moved = mm(turn_ref[...], grouped[:, 16 * t : 16 * t + 16].reshape(256, CHANS))
         moved = moved.astype(BF16).reshape(8, 2, 16, CHANS)
@@ -161,7 +170,7 @@
         pltpu.VMEM((512, CHANS), BF16),
         pltpu.VMEM((256, 256), BF16),
         pltpu.VMEM((256, 128), BF16),
-        pltpu.VMEM((CHANS, 3 * CHANS), BF16),
+        pltpu.VMEM((3, CHANS, CHANS), BF16),
         pltpu.VMEM((CHANS, CHANS), BF16),
     ]
 
@@ -173,7 +182,7 @@
         in_specs=[in_vmem(), *in_hbm(2), *[in_vmem() for _ in earlier]],
         out_specs=in_vmem(),
         out_shape=jax.ShapeDtypeStruct(shape, BF16),
-        scratch_shapes=[*attention_scratch(), pltpu.SemaphoreType.DMA((2,))],
+        scratch_shapes=[*attention_scratch(), pltpu.SemaphoreType.DMA((4,))],
         compiler_params=params(),
         cost_estimate=pl.CostEstimate(
             flops=8 * 1024 * CHANS * CHANS, bytes_accessed=4 * 2**20, transcendentals=2**20
@@ -232,12 +241,10 @@
             pltpu.make_async_copy(wp_hbm.at[lanes], wp_ref.at[s], sems.at[1 + s, PIECES + 1]),
         ]
 
-    for s in range(BLOCKS):
-        for piece in range(PIECES):
-            expansion(s, piece).start()
-        for copy in others(s):
-            copy.start()
-    last = fetch(sems.at[1 + BLOCKS], (xp_hbm.at[1024 * part : 1024 * part + 1024], xp_ref), (wqkv_hbm, wqkv_ref), (wo_hbm, wo_ref))
+    for piece in range(PIECES):
+        expansion(0, piece).start()
+    tokens = pltpu.make_async_copy(xp_hbm.at[1024 * part : 1024 * part + 1024], xp_ref, sems.at[0, 3])
+    last = weight_fetches(wqkv_hbm, wo_hbm, wqkv_ref, wo_ref, sems.at[1 + BLOCKS])
     turn_ref[...] = turn_matrix()
     mask_ref[...] = head_mask()
     outer[256:304] = layer_norm(left_ref[...].astype(F32))
@@ -248,6 +255,8 @@
     outer[128 - plain_at : 256 - plain_at] = mm(edge_matrix(part), source).astype(BF16)
     for copy in first[1:]:
         copy.wait()
+    for copy in others(0):
+        copy.start()
 
     sub = lax.broadcasted_iota(jnp.int32, (8, CB), 0)
 
@@ -263,19 +272,33 @@
             rim[:, at : at + 256] = made[256:352].astype(F32)
         for row in range(10):
             at = 8 * part + row
-            last = pad[row, 8].astype(F32)
-            first = pad[row, 1].astype(F32)
+            far = pad[row, 8].astype(F32)
+            near = pad[row, 1].astype(F32)
             west, east = [], []
             for b in range(2):
-                turned = pltpu.roll(last[8 * b : 8 * b + 8], 1, 0)
+                turned = pltpu.roll(far[8 * b : 8 * b + 8], 1, 0)
                 west.append(jnp.where(sub == 0, rim[at + 16 * b : at + 16 * b + 1], turned))
-                turned = pltpu.roll(first[8 * b : 8 * b + 8], 7, 0)
+                turned = pltpu.roll(near[8 * b : 8 * b + 8], 7, 0)
                 east.append(jnp.where(sub == 7, rim[at + 48 + 16 * b : at + 48 + 16 * b + 1], turned))
             pad[row, 0] = jnp.concatenate(west, axis=0).astype(BF16)
             pad[row, 9] = jnp.concatenate(east, axis=0).astype(BF16)
 
         for copy in others(s):
             copy.wait()
+
+        @pl.when(s + 1 < BLOCKS)
+        def _():
+            for piece in range(PIECES):
+                expansion(s + 1, piece).start()
+            for copy in others(s + 1):
+                copy.start()
+
+        @pl.when(s == BLOCKS - 1)
+        def _():
+            tokens.start()
+            for copy in last:
+                copy.start()
+
         taps = [[jnp.broadcast_to(dw_ref[s, a, b : b + 1].astype(BF16), (16, CB)) for b in range(3)] for a in range(3)]
 
         def pair_of_rows(pair, carry):
@@ -297,8 +320,7 @@
         return carry
 
     lax.fori_loop(0, BLOCKS, block, 0)
-    for copy in last:
-        copy.wait()
+    tokens.wait()
     for pair in range(4):
         rows = slice(256 * pair, 256 * pair + 256)
         mixed = (xp_ref[rows].astype(F32) + acc[rows]).astype(BF16)
@@ -309,7 +331,7 @@
         for i in range(8):
             out_ref[i, :, half] = rows[:, :, i].reshape(4, 16, CHANS).astype(BF16)
 
-    attention(grouped, wqkv_ref, wo_ref, mask_ref, proj, context, emit)
+    attention(grouped, wqkv_ref, wo_ref, mask_ref, proj, context, last, emit)
 
 
 def local_part(part, rims, *arrays):

time: 146 us -> 149 us (1.021)
  Pallas kernels: 57.6 us -> 60.9 us
    pallas_call x2, Pallas kernels: 38.2 us -> 41.8 us  [local_part(): pl.pallas_call(functools.partial(local_kernel, part), in_specs=[*[in_vmem...]
  transfers between devices with their start and end apart: 6 -> 6, of which waited for: 3 -> 2; matrix products, arithmetic and copies ran while one was open for 1% -> 1% of each run, Pallas kernels for 21% -> 22%
where the time goes in v2:
time: 149 us
  Pallas kernels  60.9 us (41%)
  blocking collectives  34.3 us (23%)
  starting transfers between devices  32.6 us (22%)
  waiting for transfers between devices  17 us (11%)
  local copies, waits for them, and re-layouts  3.64 us (2%)
    pallas_call x2, Pallas kernels, local_part(): pl.pallas_call(functools.partial(local_kernel, part), in_specs=[*[in_vmem...  41.8 us
    all_to_all x1, blocking collectives, exchange(): lax.all_to_all(blocks, ('row', 'col'), 0, 0, axis_index_groups=groups, ti...  34.3 us
    all_to_all x2, starting transfers between devices, exchange(): lax.all_to_all(blocks, ('row', 'col'), 0, 0, axis_index_groups=groups, ti...  24.2 us
    pallas_call x2, Pallas kernels, grid_attention(): pl.pallas_call(grid_kernel, in_specs=[in_vmem(), *in_hbm(2), *[in_vmem()...  15.2 us
    all_to_all x2, waiting for transfers between devices, exchange(): lax.all_to_all(blocks, ('row', 'col'), 0, 0, axis_index_groups=groups, ti...  12.2 us
    ppermute x1, waiting for transfers between devices, on_device(): bottom = lax.ppermute(field[0], 'row', up)  4.78 us
    ppermute x1, starting transfers between devices, on_device(): left = lax.ppermute(east, 'col', [(i, i + 1) for i in range(n_col - 1)])  4.55 us
    pallas_call x1, Pallas kernels, prepare(): pl.pallas_call(prepare_kernel, grid=(2,), in_specs=[pl.BlockSpec((2, 8, 6...  3.9 us
  transfers between devices with their start and end apart: 6, of which 2 were waited for; matrix products, arithmetic and copies ran while one was open for 1% of the time, Pallas kernels for 22%

profile of v2, /device:TPU:0, one launch (start us, length us, event | category | flops | bytes accessed | tf_op | source)
XLA Modules:
  0.0 148.7 jit_solution(4819052133868005254)
XLA Ops:
  0.0 0.9 slice_bitcast_fusion
  0.9 1.3 collective-permute-start.1
  2.2 1.3 collective-permute-start
  3.5 1.1 fusion
  4.7 0.1 pad.7.clone
  4.7 0.0 collective-permute-done.1.rim_ref
  4.7 4.8 %collective-permute-done.rim_ref = bf16[64,512]{1,0:T(8,128)(2,1)S(1)} collective-permute-done((bf16[64,512]{1,0:T(8,128)(2,1)S(1)}, bf16[64,512]{1,0:T(8,128)(2,1)S(1)}, u32[]{:S(2)}, u32[]{:S(2)}) %collective-permute-start) | collective-permute-done | bytes 65568 | tf_op jit(solution)/shard_map/ppermute | solution.py:376
  9.5 0.1 maximum_maximum_fusion.1
  9.6 1.3 collective-permute-start.3
  10.9 4.5 %collective-permute-start.2 = (bf16[48,512]{1,0:T(8,128)(2,1)S(1)}, bf16[48,512]{1,0:T(8,128)(2,1)S(1)}, u32[]{:S(2)}, u32[]{:S(2)}) collective-permute-start(bf16[48,512]{1,0:T(8,128)(2,1)S(1)} %get-tuple-element.18._), channel_id=1, source_target_pairs={{0,1},{1,2},{2,3},{3,4},{4,5},{5,6},{6,7},{7,8},{8,9},{9,10},{10,1... | collective-permute-start | bytes 147464 | tf_op jit(solution)/shard_map/ppermute | solution.py:383
  15.5 3.9 %prepare.1 = (bf16[2048,512]{1,0:T(8,128)(2,1)}, bf16[2048,512]{1,0:T(8,128)(2,1)}) custom-call(bf16[2,16,64,512]{3,2,1,0:T(8,128)(2,1)} %bitcast.20, bf16[48,512]{1,0:T(8,128)(2,1)S(1)} %get-tuple-element.18._), custom_call_target="tpu_custom_call" | custom-call | flops 10000000000 | bytes 16777216 | tf_op jit(solution)/shard_map/prepare/pallas_call | solution.py:203
  19.4 0.0 collective-permute-done.3.right_ref
  19.4 0.0 collective-permute-done.2.left_ref
  19.4 20.9 %local_part.3 = bf16[8,4,2,16,512]{4,3,2,1,0:T(8,128)(2,1)} custom-call(bf16[64,512]{1,0:T(8,128)(2,1)S(1)} %collective-permute-done.1.rim_ref, bf16[48,512]{1,0:T(8,128)(2,1)S(1)} %collective-permute-done.2.left_ref, bf16[48,512]{1,0:T(8,128)(2,1)S(1)} %collective-permute-done.3.right_ref, bf16[2048,512]{1,0:T(8,128)(2,1)} %get-tuple-element.7.normed_hbm, ...), custom_call_target="tpu_custom_call" | custom-call | flops 4294967296 | bytes 8388608 | tf_op jit(solution)/shard_map/local_part/pallas_call | solution.py:339
  40.3 14.1 %all-to-all-start.1 = ((bf16[32,2,16,512]{3,2,1,0:T(8,128)(2,1)}), bf16[32,2,16,512]{3,2,1,0:T(8,128)(2,1)S(1)}, u32[]{:S(2)}, u32[]{:S(2)}) async-start(bf16[32,2,16,512]{3,2,1,0:T(8,128)(2,1)} %bitcast.7), calls=%async_computation.1 | async-start | bytes 2097152 | tf_op jit(solution)/shard_map/all_to_all | solution.py:368
  54.4 20.9 %local_part.2 = bf16[8,4,2,16,512]{4,3,2,1,0:T(8,128)(2,1)} custom-call(bf16[64,512]{1,0:T(8,128)(2,1)S(1)} %collective-permute-done.rim_ref, bf16[48,512]{1,0:T(8,128)(2,1)S(1)} %collective-permute-done.2.left_ref, bf16[48,512]{1,0:T(8,128)(2,1)S(1)} %collective-permute-done.3.right_ref, bf16[2048,512]{1,0:T(8,128)(2,1)} %get-tuple-element.7.normed_hbm, ...), custom_call_target="tpu_custom_call" | custom-call | flops 4294967296 | bytes 8388608 | tf_op jit(solution)/shard_map/local_part/pallas_call | solution.py:339
  75.3 0.0 all-to-all-done.1
  75.3 10.0 %all-to-all-start = ((bf16[32,2,16,512]{3,2,1,0:T(8,128)(2,1)}), bf16[32,2,16,512]{3,2,1,0:T(8,128)(2,1)S(1)}, u32[]{:S(2)}, u32[]{:S(2)}) async-start(bf16[32,2,16,512]{3,2,1,0:T(8,128)(2,1)} %bitcast.5), calls=%async_computation | async-start | bytes 2097152 | tf_op jit(solution)/shard_map/all_to_all | solution.py:368
  85.4 7.6 %grid_attention.2.rest_0_ = bf16[32,2,16,512]{3,2,1,0:T(8,128)(2,1)S(1)} custom-call(bf16[64,16,512]{2,1,0:T(8,128)(2,1)S(1)} %bitcast.17, bf16[512,1536]{1,0:T(8,128)(2,1)} %wqkv_hbm.7, bf16[512,512]{1,0:T(8,128)(2,1)} %wo_hbm.7), custom_call_target="tpu_custom_call" | custom-call | flops 2147483648 | bytes 4194304 | tf_op jit(solution)/shard_map/grid_attention/pallas_call | solution.py:180
  93.0 12.2 %all-to-all-done = bf16[32,2,16,512]{3,2,1,0:T(8,128)(2,1)S(1)} async-done(((bf16[32,2,16,512]{3,2,1,0:T(8,128)(2,1)}), bf16[32,2,16,512]{3,2,1,0:T(8,128)(2,1)S(1)}, u32[]{:S(2)}, u32[]{:S(2)}) %all-to-all-start) | async-done | bytes 1048608 | tf_op jit(solution)/shard_map/all_to_all | solution.py:368
  105.2 7.6 %grid_attention.3 = bf16[32,2,2,16,512]{4,3,2,1,0:T(8,128)(2,1)S(1)} custom-call(bf16[64,16,512]{2,1,0:T(8,128)(2,1)S(1)} %bitcast.18, bf16[512,1536]{1,0:T(8,128)(2,1)} %wqkv_hbm.7, bf16[512,512]{1,0:T(8,128)(2,1)} %wo_hbm.7, bf16[32,2,16,512]{3,2,1,0:T(8,128)(2,1)S(1)} %grid_attention.2.rest_0_), custom_call_target="tpu_custom_call" | custom-call | flops 2147483648 | bytes 4194304 | tf_op jit(solution)/shard_map/grid_attention/pallas_call | solution.py:180
  112.8 34.3 %all_to_all.15 = bf16[32,2,2,16,512]{4,3,2,1,0:T(8,128)(2,1)S(1)} all-to-all(bf16[32,2,2,16,512]{4,3,2,1,0:T(8,128)(2,1)S(1)} %grid_attention.3), channel_id=1, replica_groups={{0,4,8,12,16,20,24,28,32,36,40,44,48,52,56,60,64,68,72,76,80,84,88,92,9..., dimensions={0} | all-to-all | bytes 4194304 | tf_op jit(solution)/shard_map/all_to_all | solution.py:368
  147.2 1.5 %copy.11 = bf16[2,2,8,4,16,512]{5,4,3,2,1,0:T(8,128)(2,1)} copy(bf16[2,2,8,4,16,512]{5,4,0,1,3,2:T(8,128)(2,1)S(1)} %bitcast.19) | data formatting | bytes 4194304 | tf_op jit(solution)/shard_map/transpose | solution.py:396
  (4 shorter events, 0.0 us)
Async XLA Ops:
  0.9 3.9 %collective-permute-start.1 = (bf16[64,512]{1,0:T(8,128)(2,1)S(1)}, bf16[64,512]{1,0:T(8,128)(2,1)S(1)}, u32[]{:S(2)}, u32[]{:S(2)}) collective-permute-start(bf16[64,512]{1,0:T(8,128)(2,1)S(1)} %get-tuple-element.11), channel_id=1, source_target_pairs={{0,32},{32,64},{64,96},{1,33},{33,65},{65,97},{2,34},{34,66},{66,9... | collective-permute-start | bytes 196616 | tf_op jit(solution)/shard_map/ppermute | solution.py:375
  2.2 7.3 %collective-permute-start = (bf16[64,512]{1,0:T(8,128)(2,1)S(1)}, bf16[64,512]{1,0:T(8,128)(2,1)S(1)}, u32[]{:S(2)}, u32[]{:S(2)}) collective-permute-start(bf16[64,512]{1,0:T(8,128)(2,1)S(1)} %get-tuple-element.12), channel_id=1, source_target_pairs={{32,0},{64,32},{96,64},{33,1},{65,33},{97,65},{34,2},{66,34},{98,6... | collective-permute-start | bytes 196616 | tf_op jit(solution)/shard_map/ppermute | solution.py:376
  9.6 9.8 %collective-permute-start.3 = (bf16[48,512]{1,0:T(8,128)(2,1)S(1)}, bf16[48,512]{1,0:T(8,128)(2,1)S(1)}, u32[]{:S(2)}, u32[]{:S(2)}) collective-permute-start(bf16[48,512]{1,0:T(8,128)(2,1)S(1)} %get-tuple-element.17), channel_id=1, source_target_pairs={{1,0},{2,1},{3,2},{4,3},{5,4},{6,5},{7,6},{8,7},{9,8},{10,9},{11,1... | collective-permute-start | bytes 147464 | tf_op jit(solution)/shard_map/ppermute | solution.py:384
  10.9 8.5 %collective-permute-start.2 = (bf16[48,512]{1,0:T(8,128)(2,1)S(1)}, bf16[48,512]{1,0:T(8,128)(2,1)S(1)}, u32[]{:S(2)}, u32[]{:S(2)}) collective-permute-start(bf16[48,512]{1,0:T(8,128)(2,1)S(1)} %get-tuple-element.18._), channel_id=1, source_target_pairs={{0,1},{1,2},{2,3},{3,4},{4,5},{5,6},{6,7},{7,8},{8,9},{9,10},{10,1... | collective-permute-start | bytes 147464 | tf_op jit(solution)/shard_map/ppermute | solution.py:383
  40.3 35.0 %all-to-all-start.1 = ((bf16[32,2,16,512]{3,2,1,0:T(8,128)(2,1)}), bf16[32,2,16,512]{3,2,1,0:T(8,128)(2,1)S(1)}, u32[]{:S(2)}, u32[]{:S(2)}) async-start(bf16[32,2,16,512]{3,2,1,0:T(8,128)(2,1)} %bitcast.7), calls=%async_computation.1 | async-start | bytes 2097152 | tf_op jit(solution)/shard_map/all_to_all | solution.py:368
  75.3 29.8 %all-to-all-start = ((bf16[32,2,16,512]{3,2,1,0:T(8,128)(2,1)}), bf16[32,2,16,512]{3,2,1,0:T(8,128)(2,1)S(1)}, u32[]{:S(2)}, u32[]{:S(2)}) async-start(bf16[32,2,16,512]{3,2,1,0:T(8,128)(2,1)} %bitcast.5), calls=%async_computation | async-start | bytes 2097152 | tf_op jit(solution)/shard_map/all_to_all | solution.py:368

commit v3 on v1

--- a/solution.py
+++ b/solution.py
@@ -16,7 +16,6 @@
 CB = 1024
 BLOCKS = WIDE // CB
 PAIRS = 4
-PIECES = CB // 256
 VMEM_LIMIT = 36 * 2**20
 SCALE_LOG2 = float(HEAD**-0.5 * np.log2(np.e))
 
@@ -221,22 +220,15 @@
         (normed_hbm.at[128 * plain : 128 * plain + 128], outer.at[plain_at : plain_at + 128]),
     )
 
-    def expansion(s, piece):
-        lanes = pl.ds(pl.multiple_of(CB * s + 256 * piece, 256), 256)
-        return pltpu.make_async_copy(we_hbm.at[:, lanes], we_ref.at[s, piece], sems.at[1 + s, piece])
-
-    def others(s):
-        lanes = pl.ds(pl.multiple_of(CB * s, CB), CB)
-        return [
-            pltpu.make_async_copy(dw_hbm.at[:, :, lanes], dw_ref.at[s], sems.at[1 + s, PIECES]),
-            pltpu.make_async_copy(wp_hbm.at[lanes], wp_ref.at[s], sems.at[1 + s, PIECES + 1]),
-        ]
-
+    blocks = []
     for s in range(BLOCKS):
-        for piece in range(PIECES):
-            expansion(s, piece).start()
-        for copy in others(s):
-            copy.start()
+        lanes = slice(CB * s, CB * s + CB)
+        blocks += fetch(
+            sems.at[1 + s],
+            (we_hbm.at[:, lanes], we_ref.at[s]),
+            (dw_hbm.at[:, :, lanes], dw_ref.at[s]),
+            (wp_hbm.at[lanes], wp_ref.at[s]),
+        )
     last = fetch(sems.at[1 + BLOCKS], (xp_hbm.at[1024 * part : 1024 * part + 1024], xp_ref), (wqkv_hbm, wqkv_ref), (wo_hbm, wo_ref))
     turn_ref[...] = turn_matrix()
     mask_ref[...] = head_mask()
@@ -246,18 +238,16 @@
     first[0].wait()
     source = jnp.concatenate([special_ref[...], layer_norm(rim_ref[...].astype(F32))], axis=0)
     outer[128 - plain_at : 256 - plain_at] = mm(edge_matrix(part), source).astype(BF16)
-    for copy in first[1:]:
+    for copy in (*first[1:], *blocks):
         copy.wait()
 
     sub = lax.broadcasted_iota(jnp.int32, (8, CB), 0)
 
     def block(s, carry):
-        for piece in range(PIECES):
-            at = 256 * piece
-            expansion(s, piece).wait()
-            made = gelu(mm(normed_ref[...], we_ref[s, piece])).astype(BF16)
+        for at in range(0, CB, 256):
+            made = gelu(mm(normed_ref[...], we_ref[s, :, at : at + 256])).astype(BF16)
             pad[1:9, 1:9, :, at : at + 256] = made.reshape(8, 8, 16, 256)
-            made = gelu(mm(outer[...], we_ref[s, piece])).astype(BF16)
+            made = gelu(mm(outer[...], we_ref[s, :, at : at + 256])).astype(BF16)
             pad[0, 1:9, :, at : at + 256] = made[0:128].reshape(8, 16, 256)
             pad[9, 1:9, :, at : at + 256] = made[128:256].reshape(8, 16, 256)
             rim[:, at : at + 256] = made[256:352].astype(F32)
@@ -274,8 +264,6 @@
             pad[row, 0] = jnp.concatenate(west, axis=0).astype(BF16)
             pad[row, 9] = jnp.concatenate(east, axis=0).astype(BF16)
 
-        for copy in others(s):
-            copy.wait()
         taps = [[jnp.broadcast_to(dw_ref[s, a, b : b + 1].astype(BF16), (16, CB)) for b in range(3)] for a in range(3)]
 
         def pair_of_rows(pair, carry):
@@ -324,7 +312,7 @@
             pltpu.VMEM((352, CHANS), BF16),
             pltpu.VMEM((128, CHANS), BF16),
             pltpu.VMEM((1024, CHANS), BF16),
-            pltpu.VMEM((BLOCKS, PIECES, CHANS, 256), BF16),
+            pltpu.VMEM((BLOCKS, CHANS, CB), BF16),
             pltpu.VMEM((BLOCKS, 3, 3, CB), F32),
             pltpu.VMEM((BLOCKS, CB, CHANS), BF16),
             pltpu.VMEM((10, 10, 16, CB), BF16),
@@ -332,7 +320,7 @@
             pltpu.VMEM((8, 8, 16, CB), BF16),
             pltpu.VMEM((1024, CHANS), F32),
             *attention_scratch(),
-            pltpu.SemaphoreType.DMA((2 + BLOCKS, PIECES + 2)),
+            pltpu.SemaphoreType.DMA((2 + BLOCKS, 3)),
         ],
         compiler_params=params(),
         cost_estimate=pl.CostEstimate(

time: 146 us -> 143 us (0.979)
  Pallas kernels: 57.6 us -> 55.4 us
    pallas_call x2, Pallas kernels: 38.2 us -> 36 us  [local_part(): pl.pallas_call(functools.partial(local_kernel, part), in_specs=[*[in_vmem...]
where the time goes in v3:
time: 143 us
  Pallas kernels  55.4 us (39%)
  blocking collectives  34.3 us (24%)
  starting transfers between devices  30.6 us (21%)
  waiting for transfers between devices  18.7 us (13%)
  local copies, waits for them, and re-layouts  3.64 us (3%)
    pallas_call x2, Pallas kernels, local_part(): pl.pallas_call(functools.partial(local_kernel, part), in_specs=[*[in_vmem...  36 us
    all_to_all x1, blocking collectives, exchange(): lax.all_to_all(blocks, ('row', 'col'), 0, 0, axis_index_groups=groups, ti...  34.3 us
    all_to_all x2, starting transfers between devices, exchange(): lax.all_to_all(blocks, ('row', 'col'), 0, 0, axis_index_groups=groups, ti...  22.2 us
    pallas_call x2, Pallas kernels, grid_attention(): pl.pallas_call(grid_kernel, in_specs=[in_vmem(), *in_hbm(2), *[in_vmem()...  15.5 us
    all_to_all x2, waiting for transfers between devices, exchange(): lax.all_to_all(blocks, ('row', 'col'), 0, 0, axis_index_groups=groups, ti...  13.9 us
    ppermute x1, waiting for transfers between devices, on_device(): bottom = lax.ppermute(field[0], 'row', up)  4.78 us
    ppermute x1, starting transfers between devices, on_device(): left = lax.ppermute(east, 'col', [(i, i + 1) for i in range(n_col - 1)])  4.55 us
    pallas_call x1, Pallas kernels, prepare(): pl.pallas_call(prepare_kernel, grid=(2,), in_specs=[pl.BlockSpec((2, 8, 6...  3.9 us
  transfers between devices with their start and end apart: 6, of which 3 were waited for; matrix products, arithmetic and copies ran while one was open for 1% of the time, Pallas kernels for 21%

profile of v3, /device:TPU:0, one launch (start us, length us, event | category | flops | bytes accessed | tf_op | source)
XLA Modules:
  0.0 142.8 jit_solution(10627872080478345552)
XLA Ops:
  0.0 0.9 slice_bitcast_fusion
  0.9 1.3 collective-permute-start.1
  2.2 1.3 collective-permute-start
  3.5 1.1 fusion
  4.7 0.1 pad.7.clone
  4.7 0.0 collective-permute-done.1.rim_ref
  4.7 4.8 %collective-permute-done.rim_ref = bf16[64,512]{1,0:T(8,128)(2,1)S(1)} collective-permute-done((bf16[64,512]{1,0:T(8,128)(2,1)S(1)}, bf16[64,512]{1,0:T(8,128)(2,1)S(1)}, u32[]{:S(2)}, u32[]{:S(2)}) %collective-permute-start) | collective-permute-done | bytes 65568 | tf_op jit(solution)/shard_map/ppermute | solution.py:342
  9.5 0.1 maximum_maximum_fusion.1
  9.6 1.3 collective-permute-start.3
  10.9 4.5 %collective-permute-start.2 = (bf16[48,512]{1,0:T(8,128)(2,1)S(1)}, bf16[48,512]{1,0:T(8,128)(2,1)S(1)}, u32[]{:S(2)}, u32[]{:S(2)}) collective-permute-start(bf16[48,512]{1,0:T(8,128)(2,1)S(1)} %get-tuple-element.18._), channel_id=1, source_target_pairs={{0,1},{1,2},{2,3},{3,4},{4,5},{5,6},{6,7},{7,8},{8,9},{9,10},{10,1... | collective-permute-start | bytes 147464 | tf_op jit(solution)/shard_map/ppermute | solution.py:349
  15.5 3.9 %prepare.1 = (bf16[2048,512]{1,0:T(8,128)(2,1)}, bf16[2048,512]{1,0:T(8,128)(2,1)}) custom-call(bf16[2,16,64,512]{3,2,1,0:T(8,128)(2,1)} %bitcast.20, bf16[48,512]{1,0:T(8,128)(2,1)S(1)} %get-tuple-element.18._), custom_call_target="tpu_custom_call" | custom-call | flops 10000000000 | bytes 16777216 | tf_op jit(solution)/shard_map/prepare/pallas_call | solution.py:193
  19.4 0.0 collective-permute-done.3.right_ref
  19.4 0.0 collective-permute-done.2.left_ref
  19.4 18.0 %local_part.3 = bf16[8,4,2,16,512]{4,3,2,1,0:T(8,128)(2,1)} custom-call(bf16[64,512]{1,0:T(8,128)(2,1)S(1)} %collective-permute-done.1.rim_ref, bf16[48,512]{1,0:T(8,128)(2,1)S(1)} %collective-permute-done.2.left_ref, bf16[48,512]{1,0:T(8,128)(2,1)S(1)} %collective-permute-done.3.right_ref, bf16[2048,512]{1,0:T(8,128)(2,1)} %get-tuple-element.7.normed_hbm, ...), custom_call_target="tpu_custom_call" | custom-call | flops 4294967296 | bytes 8388608 | tf_op jit(solution)/shard_map/local_part/pallas_call | solution.py:305
  37.4 14.1 %all-to-all-start.1 = ((bf16[32,2,16,512]{3,2,1,0:T(8,128)(2,1)}), bf16[32,2,16,512]{3,2,1,0:T(8,128)(2,1)S(1)}, u32[]{:S(2)}, u32[]{:S(2)}) async-start(bf16[32,2,16,512]{3,2,1,0:T(8,128)(2,1)} %bitcast.7), calls=%async_computation.1 | async-start | bytes 2097152 | tf_op jit(solution)/shard_map/all_to_all | solution.py:334
  51.5 18.0 %local_part.2 = bf16[8,4,2,16,512]{4,3,2,1,0:T(8,128)(2,1)} custom-call(bf16[64,512]{1,0:T(8,128)(2,1)S(1)} %collective-permute-done.rim_ref, bf16[48,512]{1,0:T(8,128)(2,1)S(1)} %collective-permute-done.2.left_ref, bf16[48,512]{1,0:T(8,128)(2,1)S(1)} %collective-permute-done.3.right_ref, bf16[2048,512]{1,0:T(8,128)(2,1)} %get-tuple-element.7.normed_hbm, ...), custom_call_target="tpu_custom_call" | custom-call | flops 4294967296 | bytes 8388608 | tf_op jit(solution)/shard_map/local_part/pallas_call | solution.py:305
  69.5 1.9 %all-to-all-done.1 = bf16[32,2,16,512]{3,2,1,0:T(8,128)(2,1)S(1)} async-done(((bf16[32,2,16,512]{3,2,1,0:T(8,128)(2,1)}), bf16[32,2,16,512]{3,2,1,0:T(8,128)(2,1)S(1)}, u32[]{:S(2)}, u32[]{:S(2)}) %all-to-all-start.1) | async-done | bytes 1048608 | tf_op jit(solution)/shard_map/all_to_all | solution.py:334
  71.4 8.0 %all-to-all-start = ((bf16[32,2,16,512]{3,2,1,0:T(8,128)(2,1)}), bf16[32,2,16,512]{3,2,1,0:T(8,128)(2,1)S(1)}, u32[]{:S(2)}, u32[]{:S(2)}) async-start(bf16[32,2,16,512]{3,2,1,0:T(8,128)(2,1)} %bitcast.5), calls=%async_computation | async-start | bytes 2097152 | tf_op jit(solution)/shard_map/all_to_all | solution.py:334
  79.4 7.7 %grid_attention.2.rest_0_ = bf16[32,2,16,512]{3,2,1,0:T(8,128)(2,1)S(1)} custom-call(bf16[64,16,512]{2,1,0:T(8,128)(2,1)S(1)} %bitcast.17, bf16[512,1536]{1,0:T(8,128)(2,1)} %wqkv_hbm.7, bf16[512,512]{1,0:T(8,128)(2,1)} %wo_hbm.7), custom_call_target="tpu_custom_call" | custom-call | flops 2147483648 | bytes 4194304 | tf_op jit(solution)/shard_map/grid_attention/pallas_call | solution.py:170
  87.2 12.1 %all-to-all-done = bf16[32,2,16,512]{3,2,1,0:T(8,128)(2,1)S(1)} async-done(((bf16[32,2,16,512]{3,2,1,0:T(8,128)(2,1)}), bf16[32,2,16,512]{3,2,1,0:T(8,128)(2,1)S(1)}, u32[]{:S(2)}, u32[]{:S(2)}) %all-to-all-start) | async-done | bytes 1048608 | tf_op jit(solution)/shard_map/all_to_all | solution.py:334
  99.2 7.7 %grid_attention.3 = bf16[32,2,2,16,512]{4,3,2,1,0:T(8,128)(2,1)S(1)} custom-call(bf16[64,16,512]{2,1,0:T(8,128)(2,1)S(1)} %bitcast.18, bf16[512,1536]{1,0:T(8,128)(2,1)} %wqkv_hbm.7, bf16[512,512]{1,0:T(8,128)(2,1)} %wo_hbm.7, bf16[32,2,16,512]{3,2,1,0:T(8,128)(2,1)S(1)} %grid_attention.2.rest_0_), custom_call_target="tpu_custom_call" | custom-call | flops 2147483648 | bytes 4194304 | tf_op jit(solution)/shard_map/grid_attention/pallas_call | solution.py:170
  106.9 34.3 %all_to_all.15 = bf16[32,2,2,16,512]{4,3,2,1,0:T(8,128)(2,1)S(1)} all-to-all(bf16[32,2,2,16,512]{4,3,2,1,0:T(8,128)(2,1)S(1)} %grid_attention.3), channel_id=1, replica_groups={{0,4,8,12,16,20,24,28,32,36,40,44,48,52,56,60,64,68,72,76,80,84,88,92,9..., dimensions={0} | all-to-all | bytes 4194304 | tf_op jit(solution)/shard_map/all_to_all | solution.py:334
  141.3 1.5 %copy.11 = bf16[2,2,8,4,16,512]{5,4,3,2,1,0:T(8,128)(2,1)} copy(bf16[2,2,8,4,16,512]{5,4,0,1,3,2:T(8,128)(2,1)S(1)} %bitcast.19) | data formatting | bytes 4194304 | tf_op jit(solution)/shard_map/transpose | solution.py:362
  (4 shorter events, 0.0 us)
Async XLA Ops:
  0.9 3.9 %collective-permute-start.1 = (bf16[64,512]{1,0:T(8,128)(2,1)S(1)}, bf16[64,512]{1,0:T(8,128)(2,1)S(1)}, u32[]{:S(2)}, u32[]{:S(2)}) collective-permute-start(bf16[64,512]{1,0:T(8,128)(2,1)S(1)} %get-tuple-element.11), channel_id=1, source_target_pairs={{0,32},{32,64},{64,96},{1,33},{33,65},{65,97},{2,34},{34,66},{66,9... | collective-permute-start | bytes 196616 | tf_op jit(solution)/shard_map/ppermute | solution.py:341
  2.2 7.3 %collective-permute-start = (bf16[64,512]{1,0:T(8,128)(2,1)S(1)}, bf16[64,512]{1,0:T(8,128)(2,1)S(1)}, u32[]{:S(2)}, u32[]{:S(2)}) collective-permute-start(bf16[64,512]{1,0:T(8,128)(2,1)S(1)} %get-tuple-element.12), channel_id=1, source_target_pairs={{32,0},{64,32},{96,64},{33,1},{65,33},{97,65},{34,2},{66,34},{98,6... | collective-permute-start | bytes 196616 | tf_op jit(solution)/shard_map/ppermute | solution.py:342
  9.6 9.8 %collective-permute-start.3 = (bf16[48,512]{1,0:T(8,128)(2,1)S(1)}, bf16[48,512]{1,0:T(8,128)(2,1)S(1)}, u32[]{:S(2)}, u32[]{:S(2)}) collective-permute-start(bf16[48,512]{1,0:T(8,128)(2,1)S(1)} %get-tuple-element.17), channel_id=1, source_target_pairs={{1,0},{2,1},{3,2},{4,3},{5,4},{6,5},{7,6},{8,7},{9,8},{10,9},{11,1... | collective-permute-start | bytes 147464 | tf_op jit(solution)/shard_map/ppermute | solution.py:350
  10.9 8.5 %collective-permute-start.2 = (bf16[48,512]{1,0:T(8,128)(2,1)S(1)}, bf16[48,512]{1,0:T(8,128)(2,1)S(1)}, u32[]{:S(2)}, u32[]{:S(2)}) collective-permute-start(bf16[48,512]{1,0:T(8,128)(2,1)S(1)} %get-tuple-element.18._), channel_id=1, source_target_pairs={{0,1},{1,2},{2,3},{3,4},{4,5},{5,6},{6,7},{7,8},{8,9},{9,10},{10,1... | collective-permute-start | bytes 147464 | tf_op jit(solution)/shard_map/ppermute | solution.py:349
  37.4 34.0 %all-to-all-start.1 = ((bf16[32,2,16,512]{3,2,1,0:T(8,128)(2,1)}), bf16[32,2,16,512]{3,2,1,0:T(8,128)(2,1)S(1)}, u32[]{:S(2)}, u32[]{:S(2)}) async-start(bf16[32,2,16,512]{3,2,1,0:T(8,128)(2,1)} %bitcast.7), calls=%async_computation.1 | async-start | bytes 2097152 | tf_op jit(solution)/shard_map/all_to_all | solution.py:334
  71.4 27.8 %all-to-all-start = ((bf16[32,2,16,512]{3,2,1,0:T(8,128)(2,1)}), bf16[32,2,16,512]{3,2,1,0:T(8,128)(2,1)S(1)}, u32[]{:S(2)}, u32[]{:S(2)}) async-start(bf16[32,2,16,512]{3,2,1,0:T(8,128)(2,1)} %bitcast.5), calls=%async_computation | async-start | bytes 2097152 | tf_op jit(solution)/shard_map/all_to_all | solution.py:334

commit v4 on v3

--- a/solution.py
+++ b/solution.py
@@ -229,7 +229,6 @@
             (dw_hbm.at[:, :, lanes], dw_ref.at[s]),
             (wp_hbm.at[lanes], wp_ref.at[s]),
         )
-    last = fetch(sems.at[1 + BLOCKS], (xp_hbm.at[1024 * part : 1024 * part + 1024], xp_ref), (wqkv_hbm, wqkv_ref), (wo_hbm, wo_ref))
     turn_ref[...] = turn_matrix()
     mask_ref[...] = head_mask()
     outer[256:304] = layer_norm(left_ref[...].astype(F32))
@@ -240,6 +239,12 @@
     outer[128 - plain_at : 256 - plain_at] = mm(edge_matrix(part), source).astype(BF16)
     for copy in (*first[1:], *blocks):
         copy.wait()
+    last = fetch(
+        sems.at[1 + BLOCKS],
+        (xp_hbm.at[1024 * part : 1024 * part + 1024], xp_ref),
+        (wqkv_hbm, wqkv_ref),
+        (wo_hbm, wo_ref),
+    )
 
     sub = lax.broadcasted_iota(jnp.int32, (8, CB), 0)
 
@@ -253,13 +258,13 @@
             rim[:, at : at + 256] = made[256:352].astype(F32)
         for row in range(10):
             at = 8 * part + row
-            last = pad[row, 8].astype(F32)
-            first = pad[row, 1].astype(F32)
+            far = pad[row, 8].astype(F32)
+            near = pad[row, 1].astype(F32)
             west, east = [], []
             for b in range(2):
-                turned = pltpu.roll(last[8 * b : 8 * b + 8], 1, 0)
+                turned = pltpu.roll(far[8 * b : 8 * b + 8], 1, 0)
                 west.append(jnp.where(sub == 0, rim[at + 16 * b : at + 16 * b + 1], turned))
-                turned = pltpu.roll(first[8 * b : 8 * b + 8], 7, 0)
+                turned = pltpu.roll(near[8 * b : 8 * b + 8], 7, 0)
                 east.append(jnp.where(sub == 7, rim[at + 48 + 16 * b : at + 48 + 16 * b + 1], turned))
             pad[row, 0] = jnp.concatenate(west, axis=0).astype(BF16)
             pad[row, 9] = jnp.concatenate(east, axis=0).astype(BF16)
@@ -276,7 +281,7 @@
                         for a in range(3)
                     ]
                     total = sums[0] + sums[1] + sums[2]
-                    spatial[2 * pair + i, j] = gelu(total.astype(F32)).astype(BF16)
+                    spatial[2 * pair + i, j] = gelu(total)
             rows = pl.ds(pl.multiple_of(256 * pair, 256), 256)
             acc[rows] += mm(spatial[pl.ds(2 * pair, 2)].reshape(256, CB), wp_ref[s])
             return carry

time: 143 us -> 142 us (level)
  Pallas kernels: 55.4 us -> 53.6 us
    pallas_call x2, Pallas kernels: 36 us -> 34.3 us  [local_part(): pl.pallas_call(functools.partial(local_kernel, part), in_specs=[*[in_vmem...]
  transfers between devices with their start and end apart: 6 -> 6, of which waited for: 3 -> 3; matrix products, arithmetic and copies ran while one was open for 1% -> 1% of each run, Pallas kernels for 21% -> 20%
where the time goes in v4:
time: 142 us; the launch traced here: 141 us
  Pallas kernels  53.6 us (38%)
  blocking collectives  34.3 us (24%)
  starting transfers between devices  29.7 us (21%)
  waiting for transfers between devices  19.5 us (14%)
  local copies, waits for them, and re-layouts  3.64 us (3%)
    all_to_all x1, blocking collectives, exchange(): lax.all_to_all(blocks, ('row', 'col'), 0, 0, axis_index_groups=groups, ti...  34.3 us
    pallas_call x2, Pallas kernels, local_part(): pl.pallas_call(functools.partial(local_kernel, part), in_specs=[*[in_vmem...  34.3 us
    all_to_all x2, starting transfers between devices, exchange(): lax.all_to_all(blocks, ('row', 'col'), 0, 0, axis_index_groups=groups, ti...  21.3 us
    pallas_call x2, Pallas kernels, grid_attention(): pl.pallas_call(grid_kernel, in_specs=[in_vmem(), *in_hbm(2), *[in_vmem()...  15.5 us
    all_to_all x2, waiting for transfers between devices, exchange(): lax.all_to_all(blocks, ('row', 'col'), 0, 0, axis_index_groups=groups, ti...  14.7 us
    ppermute x1, waiting for transfers between devices, on_device(): bottom = lax.ppermute(field[0], 'row', up)  4.78 us
    ppermute x1, starting transfers between devices, on_device(): left = lax.ppermute(east, 'col', [(i, i + 1) for i in range(n_col - 1)])  4.55 us
    pallas_call x1, Pallas kernels, prepare(): pl.pallas_call(prepare_kernel, grid=(2,), in_specs=[pl.BlockSpec((2, 8, 6...  3.9 us
  transfers between devices with their start and end apart: 6, of which 3 were waited for; matrix products, arithmetic and copies ran while one was open for 1% of the time, Pallas kernels for 20%

profile of v4, /device:TPU:0, one launch (start us, length us, event | category | flops | bytes accessed | tf_op | source)
XLA Modules:
  0.0 141.1 jit_solution(15513847026553061316)
XLA Ops:
  0.0 0.9 slice_bitcast_fusion
  0.9 1.3 collective-permute-start.1
  2.2 1.3 collective-permute-start
  3.5 1.1 fusion
  4.7 0.1 pad.7.clone
  4.7 0.0 collective-permute-done.1.rim_ref
  4.7 4.8 %collective-permute-done.rim_ref = bf16[64,512]{1,0:T(8,128)(2,1)S(1)} collective-permute-done((bf16[64,512]{1,0:T(8,128)(2,1)S(1)}, bf16[64,512]{1,0:T(8,128)(2,1)S(1)}, u32[]{:S(2)}, u32[]{:S(2)}) %collective-permute-start) | collective-permute-done | bytes 65568 | tf_op jit(solution)/shard_map/ppermute | solution.py:347
  9.5 0.1 maximum_maximum_fusion.1
  9.6 1.3 collective-permute-start.3
  10.9 4.5 %collective-permute-start.2 = (bf16[48,512]{1,0:T(8,128)(2,1)S(1)}, bf16[48,512]{1,0:T(8,128)(2,1)S(1)}, u32[]{:S(2)}, u32[]{:S(2)}) collective-permute-start(bf16[48,512]{1,0:T(8,128)(2,1)S(1)} %get-tuple-element.18._), channel_id=1, source_target_pairs={{0,1},{1,2},{2,3},{3,4},{4,5},{5,6},{6,7},{7,8},{8,9},{9,10},{10,1... | collective-permute-start | bytes 147464 | tf_op jit(solution)/shard_map/ppermute | solution.py:354
  15.5 3.9 %prepare.1 = (bf16[2048,512]{1,0:T(8,128)(2,1)}, bf16[2048,512]{1,0:T(8,128)(2,1)}) custom-call(bf16[2,16,64,512]{3,2,1,0:T(8,128)(2,1)} %bitcast.20, bf16[48,512]{1,0:T(8,128)(2,1)S(1)} %get-tuple-element.18._), custom_call_target="tpu_custom_call" | custom-call | flops 10000000000 | bytes 16777216 | tf_op jit(solution)/shard_map/prepare/pallas_call | solution.py:193
  19.4 0.0 collective-permute-done.3.right_ref
  19.4 0.0 collective-permute-done.2.left_ref
  19.4 17.1 %local_part.3 = bf16[8,4,2,16,512]{4,3,2,1,0:T(8,128)(2,1)} custom-call(bf16[64,512]{1,0:T(8,128)(2,1)S(1)} %collective-permute-done.1.rim_ref, bf16[48,512]{1,0:T(8,128)(2,1)S(1)} %collective-permute-done.2.left_ref, bf16[48,512]{1,0:T(8,128)(2,1)S(1)} %collective-permute-done.3.right_ref, bf16[2048,512]{1,0:T(8,128)(2,1)} %get-tuple-element.7.normed_hbm, ...), custom_call_target="tpu_custom_call" | custom-call | flops 4294967296 | bytes 8388608 | tf_op jit(solution)/shard_map/local_part/pallas_call | solution.py:310
  36.5 14.1 %all-to-all-start.1 = ((bf16[32,2,16,512]{3,2,1,0:T(8,128)(2,1)}), bf16[32,2,16,512]{3,2,1,0:T(8,128)(2,1)S(1)}, u32[]{:S(2)}, u32[]{:S(2)}) async-start(bf16[32,2,16,512]{3,2,1,0:T(8,128)(2,1)} %bitcast.7), calls=%async_computation.1 | async-start | bytes 2097152 | tf_op jit(solution)/shard_map/all_to_all | solution.py:339
  50.7 17.1 %local_part.2 = bf16[8,4,2,16,512]{4,3,2,1,0:T(8,128)(2,1)} custom-call(bf16[64,512]{1,0:T(8,128)(2,1)S(1)} %collective-permute-done.rim_ref, bf16[48,512]{1,0:T(8,128)(2,1)S(1)} %collective-permute-done.2.left_ref, bf16[48,512]{1,0:T(8,128)(2,1)S(1)} %collective-permute-done.3.right_ref, bf16[2048,512]{1,0:T(8,128)(2,1)} %get-tuple-element.7.normed_hbm, ...), custom_call_target="tpu_custom_call" | custom-call | flops 4294967296 | bytes 8388608 | tf_op jit(solution)/shard_map/local_part/pallas_call | solution.py:310
  67.8 2.7 %all-to-all-done.1 = bf16[32,2,16,512]{3,2,1,0:T(8,128)(2,1)S(1)} async-done(((bf16[32,2,16,512]{3,2,1,0:T(8,128)(2,1)}), bf16[32,2,16,512]{3,2,1,0:T(8,128)(2,1)S(1)}, u32[]{:S(2)}, u32[]{:S(2)}) %all-to-all-start.1) | async-done | bytes 1048608 | tf_op jit(solution)/shard_map/all_to_all | solution.py:339
  70.5 7.2 %all-to-all-start = ((bf16[32,2,16,512]{3,2,1,0:T(8,128)(2,1)}), bf16[32,2,16,512]{3,2,1,0:T(8,128)(2,1)S(1)}, u32[]{:S(2)}, u32[]{:S(2)}) async-start(bf16[32,2,16,512]{3,2,1,0:T(8,128)(2,1)} %bitcast.5), calls=%async_computation | async-start | bytes 2097152 | tf_op jit(solution)/shard_map/all_to_all | solution.py:339
  77.7 7.7 %grid_attention.2.rest_0_ = bf16[32,2,16,512]{3,2,1,0:T(8,128)(2,1)S(1)} custom-call(bf16[64,16,512]{2,1,0:T(8,128)(2,1)S(1)} %bitcast.17, bf16[512,1536]{1,0:T(8,128)(2,1)} %wqkv_hbm.7, bf16[512,512]{1,0:T(8,128)(2,1)} %wo_hbm.7), custom_call_target="tpu_custom_call" | custom-call | flops 2147483648 | bytes 4194304 | tf_op jit(solution)/shard_map/grid_attention/pallas_call | solution.py:170
  85.4 12.1 %all-to-all-done = bf16[32,2,16,512]{3,2,1,0:T(8,128)(2,1)S(1)} async-done(((bf16[32,2,16,512]{3,2,1,0:T(8,128)(2,1)}), bf16[32,2,16,512]{3,2,1,0:T(8,128)(2,1)S(1)}, u32[]{:S(2)}, u32[]{:S(2)}) %all-to-all-start) | async-done | bytes 1048608 | tf_op jit(solution)/shard_map/all_to_all | solution.py:339
  97.5 7.7 %grid_attention.3 = bf16[32,2,2,16,512]{4,3,2,1,0:T(8,128)(2,1)S(1)} custom-call(bf16[64,16,512]{2,1,0:T(8,128)(2,1)S(1)} %bitcast.18, bf16[512,1536]{1,0:T(8,128)(2,1)} %wqkv_hbm.7, bf16[512,512]{1,0:T(8,128)(2,1)} %wo_hbm.7, bf16[32,2,16,512]{3,2,1,0:T(8,128)(2,1)S(1)} %grid_attention.2.rest_0_), custom_call_target="tpu_custom_call" | custom-call | flops 2147483648 | bytes 4194304 | tf_op jit(solution)/shard_map/grid_attention/pallas_call | solution.py:170
  105.2 34.3 %all_to_all.15 = bf16[32,2,2,16,512]{4,3,2,1,0:T(8,128)(2,1)S(1)} all-to-all(bf16[32,2,2,16,512]{4,3,2,1,0:T(8,128)(2,1)S(1)} %grid_attention.3), channel_id=1, replica_groups={{0,4,8,12,16,20,24,28,32,36,40,44,48,52,56,60,64,68,72,76,80,84,88,92,9..., dimensions={0} | all-to-all | bytes 4194304 | tf_op jit(solution)/shard_map/all_to_all | solution.py:339
  139.6 1.5 %copy.11 = bf16[2,2,8,4,16,512]{5,4,3,2,1,0:T(8,128)(2,1)} copy(bf16[2,2,8,4,16,512]{5,4,0,1,3,2:T(8,128)(2,1)S(1)} %bitcast.19) | data formatting | bytes 4194304 | tf_op jit(solution)/shard_map/transpose | solution.py:367
  (4 shorter events, 0.0 us)
Async XLA Ops:
  0.9 3.9 %collective-permute-start.1 = (bf16[64,512]{1,0:T(8,128)(2,1)S(1)}, bf16[64,512]{1,0:T(8,128)(2,1)S(1)}, u32[]{:S(2)}, u32[]{:S(2)}) collective-permute-start(bf16[64,512]{1,0:T(8,128)(2,1)S(1)} %get-tuple-element.11), channel_id=1, source_target_pairs={{0,32},{32,64},{64,96},{1,33},{33,65},{65,97},{2,34},{34,66},{66,9... | collective-permute-start | bytes 196616 | tf_op jit(solution)/shard_map/ppermute | solution.py:346
  2.2 7.3 %collective-permute-start = (bf16[64,512]{1,0:T(8,128)(2,1)S(1)}, bf16[64,512]{1,0:T(8,128)(2,1)S(1)}, u32[]{:S(2)}, u32[]{:S(2)}) collective-permute-start(bf16[64,512]{1,0:T(8,128)(2,1)S(1)} %get-tuple-element.12), channel_id=1, source_target_pairs={{32,0},{64,32},{96,64},{33,1},{65,33},{97,65},{34,2},{66,34},{98,6... | collective-permute-start | bytes 196616 | tf_op jit(solution)/shard_map/ppermute | solution.py:347
  9.6 9.8 %collective-permute-start.3 = (bf16[48,512]{1,0:T(8,128)(2,1)S(1)}, bf16[48,512]{1,0:T(8,128)(2,1)S(1)}, u32[]{:S(2)}, u32[]{:S(2)}) collective-permute-start(bf16[48,512]{1,0:T(8,128)(2,1)S(1)} %get-tuple-element.17), channel_id=1, source_target_pairs={{1,0},{2,1},{3,2},{4,3},{5,4},{6,5},{7,6},{8,7},{9,8},{10,9},{11,1... | collective-permute-start | bytes 147464 | tf_op jit(solution)/shard_map/ppermute | solution.py:355
  10.9 8.5 %collective-permute-start.2 = (bf16[48,512]{1,0:T(8,128)(2,1)S(1)}, bf16[48,512]{1,0:T(8,128)(2,1)S(1)}, u32[]{:S(2)}, u32[]{:S(2)}) collective-permute-start(bf16[48,512]{1,0:T(8,128)(2,1)S(1)} %get-tuple-element.18._), channel_id=1, source_target_pairs={{0,1},{1,2},{2,3},{3,4},{4,5},{5,6},{6,7},{7,8},{8,9},{9,10},{10,1... | collective-permute-start | bytes 147464 | tf_op jit(solution)/shard_map/ppermute | solution.py:354
  36.5 34.0 %all-to-all-start.1 = ((bf16[32,2,16,512]{3,2,1,0:T(8,128)(2,1)}), bf16[32,2,16,512]{3,2,1,0:T(8,128)(2,1)S(1)}, u32[]{:S(2)}, u32[]{:S(2)}) async-start(bf16[32,2,16,512]{3,2,1,0:T(8,128)(2,1)} %bitcast.7), calls=%async_computation.1 | async-start | bytes 2097152 | tf_op jit(solution)/shard_map/all_to_all | solution.py:339
  70.5 27.0 %all-to-all-start = ((bf16[32,2,16,512]{3,2,1,0:T(8,128)(2,1)}), bf16[32,2,16,512]{3,2,1,0:T(8,128)(2,1)S(1)}, u32[]{:S(2)}, u32[]{:S(2)}) async-start(bf16[32,2,16,512]{3,2,1,0:T(8,128)(2,1)} %bitcast.5), calls=%async_computation | async-start | bytes 2097152 | tf_op jit(solution)/shard_map/all_to_all | solution.py:339

commit v5 on v4

--- a/solution.py
+++ b/solution.py
@@ -105,7 +105,7 @@
     return jnp.concatenate(found, axis=1)
 
 
-def attention(grouped, wqkv_ref, wo_ref, mask_ref, proj, context, emit):
+def attention(grouped, wqkv_ref, wo_ref, mask_ref, proj, context, emit, unroll):
     mask = mask_ref[...]
 
     def one(half, carry):
@@ -124,7 +124,7 @@
         emit(half, x + mm(context[...], wo_ref[...]))
         return carry
 
-    lax.fori_loop(0, 2, one, 0, unroll=2)
+    lax.fori_loop(0, 2, one, 0, unroll=unroll)
 
 
 def grid_kernel(x_ref, wqkv_hbm, wo_hbm, *rest):
@@ -141,7 +141,7 @@
 
     for copy in copies:
         copy.wait()
-    attention(grouped, wqkv_ref, wo_ref, mask_ref, proj, context, emit)
+    attention(grouped, wqkv_ref, wo_ref, mask_ref, proj, context, emit, 2)
     for t in range(4):
         moved = mm(turn_ref[...], grouped[:, 16 * t : 16 * t + 16].reshape(256, CHANS))
         moved = moved.astype(BF16).reshape(8, 2, 16, CHANS)
@@ -220,15 +220,17 @@
         (normed_hbm.at[128 * plain : 128 * plain + 128], outer.at[plain_at : plain_at + 128]),
     )
 
-    blocks = []
-    for s in range(BLOCKS):
+
+    def fetch_block(s):
         lanes = slice(CB * s, CB * s + CB)
-        blocks += fetch(
+        return fetch(
             sems.at[1 + s],
             (we_hbm.at[:, lanes], we_ref.at[s]),
             (dw_hbm.at[:, :, lanes], dw_ref.at[s]),
             (wp_hbm.at[lanes], wp_ref.at[s]),
         )
+
+    blocks = [fetch_block(0)]
     turn_ref[...] = turn_matrix()
     mask_ref[...] = head_mask()
     outer[256:304] = layer_norm(left_ref[...].astype(F32))
@@ -237,22 +239,17 @@
     first[0].wait()
     source = jnp.concatenate([special_ref[...], layer_norm(rim_ref[...].astype(F32))], axis=0)
     outer[128 - plain_at : 256 - plain_at] = mm(edge_matrix(part), source).astype(BF16)
-    for copy in (*first[1:], *blocks):
+    for copy in first[1:]:
         copy.wait()
-    last = fetch(
-        sems.at[1 + BLOCKS],
-        (xp_hbm.at[1024 * part : 1024 * part + 1024], xp_ref),
-        (wqkv_hbm, wqkv_ref),
-        (wo_hbm, wo_ref),
-    )
 
     sub = lax.broadcasted_iota(jnp.int32, (8, CB), 0)
 
-    def block(s, carry):
+    def block(s):
+        blocks[s][0].wait()
         for at in range(0, CB, 256):
-            made = gelu(mm(normed_ref[...], we_ref[s, :, at : at + 256])).astype(BF16)
+            made = gelu(mm(normed_ref[...], we_ref[s, :, at : at + 256]).astype(BF16))
             pad[1:9, 1:9, :, at : at + 256] = made.reshape(8, 8, 16, 256)
-            made = gelu(mm(outer[...], we_ref[s, :, at : at + 256])).astype(BF16)
+            made = gelu(mm(outer[...], we_ref[s, :, at : at + 256]).astype(BF16))
             pad[0, 1:9, :, at : at + 256] = made[0:128].reshape(8, 16, 256)
             pad[9, 1:9, :, at : at + 256] = made[128:256].reshape(8, 16, 256)
             rim[:, at : at + 256] = made[256:352].astype(F32)
@@ -269,6 +266,10 @@
             pad[row, 0] = jnp.concatenate(west, axis=0).astype(BF16)
             pad[row, 9] = jnp.concatenate(east, axis=0).astype(BF16)
 
+        if s + 1 < BLOCKS:
+            blocks.append(fetch_block(s + 1))
+        for copy in blocks[s][1:]:
+            copy.wait()
         taps = [[jnp.broadcast_to(dw_ref[s, a, b : b + 1].astype(BF16), (16, CB)) for b in range(3)] for a in range(3)]
 
         def pair_of_rows(pair, carry):
@@ -287,9 +288,16 @@
             return carry
 
         lax.fori_loop(0, 4, pair_of_rows, 0, unroll=PAIRS)
-        return carry
-
-    lax.fori_loop(0, BLOCKS, block, 0)
+
+    for s in range(BLOCKS):
+        if s == BLOCKS - 1:
+            last = fetch(
+                sems.at[1 + BLOCKS],
+                (xp_hbm.at[1024 * part : 1024 * part + 1024], xp_ref),
+                (wqkv_hbm, wqkv_ref),
+                (wo_hbm, wo_ref),
+            )
+        block(s)
     for copy in last:
         copy.wait()
     for pair in range(4):
@@ -302,7 +310,7 @@
         for i in range(8):
             out_ref[i, :, half] = rows[:, :, i].reshape(4, 16, CHANS).astype(BF16)
 
-    attention(grouped, wqkv_ref, wo_ref, mask_ref, proj, context, emit)
+    attention(grouped, wqkv_ref, wo_ref, mask_ref, proj, context, emit, 1)
 
 
 def local_part(part, rims, *arrays):

time: 142 us -> 141 us (level)
  no operation moved by 1% of the time
where the time goes in v5:
time: 141 us
  Pallas kernels  53.1 us (38%)
  blocking collectives  34.3 us (24%)
  starting transfers between devices  29.2 us (21%)
  waiting for transfers between devices  20 us (14%)
  local copies, waits for them, and re-layouts  3.64 us (3%)
    all_to_all x1, blocking collectives, exchange(): lax.all_to_all(blocks, ('row', 'col'), 0, 0, axis_index_groups=groups, ti...  34.3 us
    pallas_call x2, Pallas kernels, local_part(): pl.pallas_call(functools.partial(local_kernel, part), in_specs=[*[in_vmem...  33.7 us
    all_to_all x2, starting transfers between devices, exchange(): lax.all_to_all(blocks, ('row', 'col'), 0, 0, axis_index_groups=groups, ti...  20.8 us
    pallas_call x2, Pallas kernels, grid_attention(): pl.pallas_call(grid_kernel, in_specs=[in_vmem(), *in_hbm(2), *[in_vmem()...  15.5 us
    all_to_all x2, waiting for transfers between devices, exchange(): lax.all_to_all(blocks, ('row', 'col'), 0, 0, axis_index_groups=groups, ti...  15.2 us
    ppermute x1, waiting for transfers between devices, on_device(): bottom = lax.ppermute(field[0], 'row', up)  4.78 us
    ppermute x1, starting transfers between devices, on_device(): left = lax.ppermute(east, 'col', [(i, i + 1) for i in range(n_col - 1)])  4.55 us
    pallas_call x1, Pallas kernels, prepare(): pl.pallas_call(prepare_kernel, grid=(2,), in_specs=[pl.BlockSpec((2, 8, 6...  3.9 us
  transfers between devices with their start and end apart: 6, of which 3 were waited for; matrix products, arithmetic and copies ran while one was open for 1% of the time, Pallas kernels for 20%

profile of v5, /device:TPU:0, one launch (start us, length us, event | category | flops | bytes accessed | tf_op | source)
XLA Modules:
  0.0 140.5 jit_solution(148097476652406109)
XLA Ops:
  0.0 0.9 slice_bitcast_fusion
  0.9 1.3 collective-permute-start.1
  2.2 1.3 collective-permute-start
  3.5 1.1 fusion
  4.7 0.1 pad.7.clone
  4.7 0.0 collective-permute-done.1.rim_ref
  4.7 4.8 %collective-permute-done.rim_ref = bf16[64,512]{1,0:T(8,128)(2,1)S(1)} collective-permute-done((bf16[64,512]{1,0:T(8,128)(2,1)S(1)}, bf16[64,512]{1,0:T(8,128)(2,1)S(1)}, u32[]{:S(2)}, u32[]{:S(2)}) %collective-permute-start) | collective-permute-done | bytes 65568 | tf_op jit(solution)/shard_map/ppermute | solution.py:355
  9.5 0.1 maximum_maximum_fusion.1
  9.6 1.3 collective-permute-start.3
  10.9 4.5 %collective-permute-start.2 = (bf16[48,512]{1,0:T(8,128)(2,1)S(1)}, bf16[48,512]{1,0:T(8,128)(2,1)S(1)}, u32[]{:S(2)}, u32[]{:S(2)}) collective-permute-start(bf16[48,512]{1,0:T(8,128)(2,1)S(1)} %get-tuple-element.18._), channel_id=1, source_target_pairs={{0,1},{1,2},{2,3},{3,4},{4,5},{5,6},{6,7},{7,8},{8,9},{9,10},{10,1... | collective-permute-start | bytes 147464 | tf_op jit(solution)/shard_map/ppermute | solution.py:362
  15.5 3.9 %prepare.1 = (bf16[2048,512]{1,0:T(8,128)(2,1)}, bf16[2048,512]{1,0:T(8,128)(2,1)}) custom-call(bf16[2,16,64,512]{3,2,1,0:T(8,128)(2,1)} %bitcast.20, bf16[48,512]{1,0:T(8,128)(2,1)S(1)} %get-tuple-element.18._), custom_call_target="tpu_custom_call" | custom-call | flops 10000000000 | bytes 16777216 | tf_op jit(solution)/shard_map/prepare/pallas_call | solution.py:193
  19.4 0.0 collective-permute-done.3.right_ref
  19.4 0.0 collective-permute-done.2.left_ref
  19.4 16.9 %local_part.3 = bf16[8,4,2,16,512]{4,3,2,1,0:T(8,128)(2,1)} custom-call(bf16[64,512]{1,0:T(8,128)(2,1)S(1)} %collective-permute-done.1.rim_ref, bf16[48,512]{1,0:T(8,128)(2,1)S(1)} %collective-permute-done.2.left_ref, bf16[48,512]{1,0:T(8,128)(2,1)S(1)} %collective-permute-done.3.right_ref, bf16[2048,512]{1,0:T(8,128)(2,1)} %get-tuple-element.7.normed_hbm, ...), custom_call_target="tpu_custom_call" | custom-call | flops 4294967296 | bytes 8388608 | tf_op jit(solution)/shard_map/local_part/pallas_call | solution.py:318
  36.3 13.9 %all-to-all-start.1 = ((bf16[32,2,16,512]{3,2,1,0:T(8,128)(2,1)}), bf16[32,2,16,512]{3,2,1,0:T(8,128)(2,1)S(1)}, u32[]{:S(2)}, u32[]{:S(2)}) async-start(bf16[32,2,16,512]{3,2,1,0:T(8,128)(2,1)} %bitcast.7), calls=%async_computation.1 | async-start | bytes 2097152 | tf_op jit(solution)/shard_map/all_to_all | solution.py:347
  50.2 16.9 %local_part.2 = bf16[8,4,2,16,512]{4,3,2,1,0:T(8,128)(2,1)} custom-call(bf16[64,512]{1,0:T(8,128)(2,1)S(1)} %collective-permute-done.rim_ref, bf16[48,512]{1,0:T(8,128)(2,1)S(1)} %collective-permute-done.2.left_ref, bf16[48,512]{1,0:T(8,128)(2,1)S(1)} %collective-permute-done.3.right_ref, bf16[2048,512]{1,0:T(8,128)(2,1)} %get-tuple-element.7.normed_hbm, ...), custom_call_target="tpu_custom_call" | custom-call | flops 4294967296 | bytes 8388608 | tf_op jit(solution)/shard_map/local_part/pallas_call | solution.py:318
  67.1 3.2 %all-to-all-done.1 = bf16[32,2,16,512]{3,2,1,0:T(8,128)(2,1)S(1)} async-done(((bf16[32,2,16,512]{3,2,1,0:T(8,128)(2,1)}), bf16[32,2,16,512]{3,2,1,0:T(8,128)(2,1)S(1)}, u32[]{:S(2)}, u32[]{:S(2)}) %all-to-all-start.1) | async-done | bytes 1048608 | tf_op jit(solution)/shard_map/all_to_all | solution.py:347
  70.2 6.9 %all-to-all-start = ((bf16[32,2,16,512]{3,2,1,0:T(8,128)(2,1)}), bf16[32,2,16,512]{3,2,1,0:T(8,128)(2,1)S(1)}, u32[]{:S(2)}, u32[]{:S(2)}) async-start(bf16[32,2,16,512]{3,2,1,0:T(8,128)(2,1)} %bitcast.5), calls=%async_computation | async-start | bytes 2097152 | tf_op jit(solution)/shard_map/all_to_all | solution.py:347
  77.1 7.7 %grid_attention.2.rest_0_ = bf16[32,2,16,512]{3,2,1,0:T(8,128)(2,1)S(1)} custom-call(bf16[64,16,512]{2,1,0:T(8,128)(2,1)S(1)} %bitcast.17, bf16[512,1536]{1,0:T(8,128)(2,1)} %wqkv_hbm.7, bf16[512,512]{1,0:T(8,128)(2,1)} %wo_hbm.7), custom_call_target="tpu_custom_call" | custom-call | flops 2147483648 | bytes 4194304 | tf_op jit(solution)/shard_map/grid_attention/pallas_call | solution.py:170
  84.9 12.1 %all-to-all-done = bf16[32,2,16,512]{3,2,1,0:T(8,128)(2,1)S(1)} async-done(((bf16[32,2,16,512]{3,2,1,0:T(8,128)(2,1)}), bf16[32,2,16,512]{3,2,1,0:T(8,128)(2,1)S(1)}, u32[]{:S(2)}, u32[]{:S(2)}) %all-to-all-start) | async-done | bytes 1048608 | tf_op jit(solution)/shard_map/all_to_all | solution.py:347
  96.9 7.7 %grid_attention.3 = bf16[32,2,2,16,512]{4,3,2,1,0:T(8,128)(2,1)S(1)} custom-call(bf16[64,16,512]{2,1,0:T(8,128)(2,1)S(1)} %bitcast.18, bf16[512,1536]{1,0:T(8,128)(2,1)} %wqkv_hbm.7, bf16[512,512]{1,0:T(8,128)(2,1)} %wo_hbm.7, bf16[32,2,16,512]{3,2,1,0:T(8,128)(2,1)S(1)} %grid_attention.2.rest_0_), custom_call_target="tpu_custom_call" | custom-call | flops 2147483648 | bytes 4194304 | tf_op jit(solution)/shard_map/grid_attention/pallas_call | solution.py:170
  104.7 34.3 %all_to_all.15 = bf16[32,2,2,16,512]{4,3,2,1,0:T(8,128)(2,1)S(1)} all-to-all(bf16[32,2,2,16,512]{4,3,2,1,0:T(8,128)(2,1)S(1)} %grid_attention.3), channel_id=1, replica_groups={{0,4,8,12,16,20,24,28,32,36,40,44,48,52,56,60,64,68,72,76,80,84,88,92,9..., dimensions={0} | all-to-all | bytes 4194304 | tf_op jit(solution)/shard_map/all_to_all | solution.py:347
  139.0 1.5 %copy.11 = bf16[2,2,8,4,16,512]{5,4,3,2,1,0:T(8,128)(2,1)} copy(bf16[2,2,8,4,16,512]{5,4,0,1,3,2:T(8,128)(2,1)S(1)} %bitcast.19) | data formatting | bytes 4194304 | tf_op jit(solution)/shard_map/transpose | solution.py:375
  (4 shorter events, 0.0 us)
Async XLA Ops:
  0.9 3.9 %collective-permute-start.1 = (bf16[64,512]{1,0:T(8,128)(2,1)S(1)}, bf16[64,512]{1,0:T(8,128)(2,1)S(1)}, u32[]{:S(2)}, u32[]{:S(2)}) collective-permute-start(bf16[64,512]{1,0:T(8,128)(2,1)S(1)} %get-tuple-element.11), channel_id=1, source_target_pairs={{0,32},{32,64},{64,96},{1,33},{33,65},{65,97},{2,34},{34,66},{66,9... | collective-permute-start | bytes 196616 | tf_op jit(solution)/shard_map/ppermute | solution.py:354
  2.2 7.3 %collective-permute-start = (bf16[64,512]{1,0:T(8,128)(2,1)S(1)}, bf16[64,512]{1,0:T(8,128)(2,1)S(1)}, u32[]{:S(2)}, u32[]{:S(2)}) collective-permute-start(bf16[64,512]{1,0:T(8,128)(2,1)S(1)} %get-tuple-element.12), channel_id=1, source_target_pairs={{32,0},{64,32},{96,64},{33,1},{65,33},{97,65},{34,2},{66,34},{98,6... | collective-permute-start | bytes 196616 | tf_op jit(solution)/shard_map/ppermute | solution.py:355
  9.6 9.8 %collective-permute-start.3 = (bf16[48,512]{1,0:T(8,128)(2,1)S(1)}, bf16[48,512]{1,0:T(8,128)(2,1)S(1)}, u32[]{:S(2)}, u32[]{:S(2)}) collective-permute-start(bf16[48,512]{1,0:T(8,128)(2,1)S(1)} %get-tuple-element.17), channel_id=1, source_target_pairs={{1,0},{2,1},{3,2},{4,3},{5,4},{6,5},{7,6},{8,7},{9,8},{10,9},{11,1... | collective-permute-start | bytes 147464 | tf_op jit(solution)/shard_map/ppermute | solution.py:363
  10.9 8.5 %collective-permute-start.2 = (bf16[48,512]{1,0:T(8,128)(2,1)S(1)}, bf16[48,512]{1,0:T(8,128)(2,1)S(1)}, u32[]{:S(2)}, u32[]{:S(2)}) collective-permute-start(bf16[48,512]{1,0:T(8,128)(2,1)S(1)} %get-tuple-element.18._), channel_id=1, source_target_pairs={{0,1},{1,2},{2,3},{3,4},{4,5},{5,6},{6,7},{7,8},{8,9},{9,10},{10,1... | collective-permute-start | bytes 147464 | tf_op jit(solution)/shard_map/ppermute | solution.py:362
  36.3 34.0 %all-to-all-start.1 = ((bf16[32,2,16,512]{3,2,1,0:T(8,128)(2,1)}), bf16[32,2,16,512]{3,2,1,0:T(8,128)(2,1)S(1)}, u32[]{:S(2)}, u32[]{:S(2)}) async-start(bf16[32,2,16,512]{3,2,1,0:T(8,128)(2,1)} %bitcast.7), calls=%async_computation.1 | async-start | bytes 2097152 | tf_op jit(solution)/shard_map/all_to_all | solution.py:347
  70.2 26.7 %all-to-all-start = ((bf16[32,2,16,512]{3,2,1,0:T(8,128)(2,1)}), bf16[32,2,16,512]{3,2,1,0:T(8,128)(2,1)S(1)}, u32[]{:S(2)}, u32[]{:S(2)}) async-start(bf16[32,2,16,512]{3,2,1,0:T(8,128)(2,1)} %bitcast.5), calls=%async_computation | async-start | bytes 2097152 | tf_op jit(solution)/shard_map/all_to_all | solution.py:347
